TPU v7x, 512 devices: a whole 4x4x16 slice. The times are simulated.
512 devices in a mesh: outer: 16 (over z), inner: 32 (over x, y, core).
Axes of the slice: x: 4, y: 4, z: 16, core: 2. Of those that a mesh axis runs over, the one named last changes fastest.
Arguments:
- queries_first: bfloat16 [8192, 32, 256], P('inner', 'outer'), may hold values from -80 to 80
- queries_second: bfloat16 [8192, 32, 256], P('inner', 'outer'), may hold values from -80 to 80
- shared_keys: bfloat16 [8192, 256], P(('inner', 'outer')), may hold values from -5 to 5
- shared_values: bfloat16 [8192, 256], P(('inner', 'outer')), may hold values from -6 to 6
Outputs:
- out_first: bfloat16 [8192, 32, 256], P('inner', 'outer')
- out_second: bfloat16 [8192, 32, 256], P('inner', 'outer')
All inputs are finite; a program needn't handle non-finite values.
Results may differ from a plain program's by a relative error of at most 0.0035.
Values may be sent and summed in bfloat16 or wider, within the bound.
A program may use at most 128 MiB of HBM per device.

v0:
```python
import math

import jax
import jax.numpy as jnp
from jax import lax
from jax.sharding import PartitionSpec as P

NEGATIVE = -1e30


def empty_state(row_count, head_width):
    return (
        jnp.full((row_count,), NEGATIVE, jnp.float32),
        jnp.zeros((row_count,), jnp.float32),
        jnp.zeros((row_count, head_width), jnp.float32),
    )


def flatten_rows(queries):
    return queries.reshape(queries.shape[0] * queries.shape[1], queries.shape[2])


def online_step(carried, query_rows, positions, last_token, pieces, key_pos):
    key_piece, value_piece = pieces
    score_scale = 1.0 / math.sqrt(query_rows.shape[1])

    def update(current):
        running_max, denominator, running_sum = current
        scores = (
            lax.dot_general(
                query_rows, key_piece, (((1,), (1,)), ((), ())), preferred_element_type=jnp.float32
            )
            * score_scale
        )
        allowed = key_pos[None, :] <= positions[:, None]
        scores = jnp.where(allowed, scores, NEGATIVE)
        new_max = jnp.maximum(running_max, jnp.max(scores, axis=1))
        weights = jnp.where(allowed, jnp.exp(scores - new_max[:, None]), 0.0)
        denominator = jnp.sum(weights, axis=1)
        running_sum = jnp.dot(
            weights.astype(jnp.bfloat16), value_piece, preferred_element_type=jnp.float32
        )
        return (new_max, denominator, running_sum)

    def keep_state(current):
        return current

    return lax.cond(jnp.min(key_pos) <= last_token, update, keep_state, carried)


def finish(carried, tokens_here, groups):
    running_max, denominator, running_sum = carried
    result = running_sum / denominator[:, None]
    return result.reshape(tokens_here, groups, running_sum.shape[1]).astype(jnp.bfloat16)


def on_device(queries_first, queries_second, shared_keys, shared_values):
    tokens_here, head_count, head_width = queries_first.shape
    inner_place = lax.axis_index("inner")
    first_token = inner_place * tokens_here
    local_rows = jnp.arange(tokens_here, dtype=jnp.int32)
    query_sets = (jnp.concatenate((queries_first, queries_second), axis=1),)
    token_list = (first_token + local_rows,)
    groups = query_sets[0].shape[1]
    members = range(len(query_sets))
    rows_list = tuple((flatten_rows(query_sets[member]) for member in members))
    position_list = tuple((jnp.repeat(token_list[member], groups) for member in members))
    last_list = tuple((jnp.max(token_list[member]) for member in members))
    initial = tuple((empty_state(tokens_here * groups, head_width) for member in members))
    block_keys, block_values = (
        lax.all_gather(shared_keys, "outer", axis=0, tiled=True),
        lax.all_gather(shared_values, "outer", axis=0, tiled=True),
    )
    pieces = (
        lax.all_gather(block_keys, "inner", axis=0, tiled=True),
        lax.all_gather(block_values, "inner", axis=0, tiled=True),
    )
    key_pos = jnp.arange(pieces[0].shape[0], dtype=jnp.int32)
    states = tuple(
        (
            online_step(
                initial[member],
                rows_list[member],
                position_list[member],
                last_list[member],
                pieces,
                key_pos,
            )
            for member in members
        )
    )
    merged = finish(states[0], tokens_here, groups)
    first_out = merged[:, :head_count]
    second_out = merged[:, head_count:]
    return (first_out, second_out)


def solution(mesh):
    return jax.shard_map(
        on_device,
        mesh=mesh,
        in_specs=(
            P("inner", "outer", None),
            P("inner", "outer", None),
            P(("inner", "outer"), None),
            P(("inner", "outer"), None),
        ),
        out_specs=(P("inner", "outer", None), P("inner", "outer", None)),
        check_vma=False,
    )
```

profile of v0, /device:TPU:6, one launch (start us, length us, event | category | flops | bytes accessed | tf_op | source)
XLA Modules:
  0.0 221.7 jit_solution(15209705383831174302)
XLA Ops:
  7.2 0.0 all-gather.3.cloned.1.call-start
  7.2 38.7 %all_gather.12 = bf16[256,256]{1,0:T(8,128)(2,1)} all-gather(bf16[16,256]{1,0:T(8,128)(2,1)} %param.8), channel_id=1, replica_groups=mesh['outer'=16,'inner'=32] {'outer'}, dimensions={0}, use_global_device_ids=true | all-gather | bytes 139264 | tf_op jit(solution)/shard_map/all_gather | solution.py:71
  45.9 0.0 all-gather.3.cloned.1.call-update
  45.9 0.0 all-gather.5.cloned.1.call-start
  46.0 29.3 %all_gather.14 = bf16[256,256]{1,0:T(8,128)(2,1)} all-gather(bf16[16,256]{1,0:T(8,128)(2,1)} %param.9), channel_id=1, replica_groups=mesh['outer'=16,'inner'=32] {'outer'}, dimensions={0}, use_global_device_ids=true | all-gather | bytes 139264 | tf_op jit(solution)/shard_map/all_gather | solution.py:72
  75.2 0.0 all-gather.5.cloned.1.call-update
  75.3 0.6 fusion.8
  76.6 1.6 pad_maximum_fusion
  78.1 24.9 %all-gather.3.cloned.1.call-done = bf16[8192,256]{1,0:T(8,128)(2,1)} async-done(((bf16[256,256]{1,0:T(8,128)(2,1)}), bf16[8192,256]{1,0:T(8,128)(2,1)}) %all-gather.3.cloned.1.call-update) | async-done | bytes 4194320 | tf_op jit(solution)/shard_map/all_gather | solution.py:75
  103.0 64.0 %all-gather.5.cloned.1.call-done = bf16[8192,256]{1,0:T(8,128)(2,1)} async-done(((bf16[256,256]{1,0:T(8,128)(2,1)}), bf16[8192,256]{1,0:T(8,128)(2,1)}) %all-gather.5.cloned.1.call-update) | async-done | bytes 4194320 | tf_op jit(solution)/shard_map/all_gather | solution.py:76
  167.1 46.3 %conditional.1 = (f32[1024]{0:T(1024)S(1)}, f32[1024,256]{1,0:T(8,128)S(1)}) conditional(s32[]{:T(128)} %convert_element_type.12, () %tuple.16, (s32[8192]{0:T(1024)S(1)}, s32[256]{0:T(256)S(1)}, bf16[256,4,256]{2,1,0:T(4,128)(2,1)S(1)}, bf16[8192,256]{1,0:T(8,128)(2,1)}, bf16[8192,256]{1,0:T(8,128)(2,1)}) %tuple.17), branch_computations={%region_1.0_spmd, %region_2.5_spmd} | conditional | flops 8724151296 | bytes 128599080 | solution.py:48
  167.1 0.1 broadcast_in_dim.19
  167.2 0.1 le.3
  167.3 0.1 reshape.15
  167.4 0.0 copy-start
  167.4 16.0 %fusion = (f32[1024]{0:T(1024)S(1)}, f32[1024,8192]{1,0:T(8,128)}) fusion(s32[8192]{0:T(1024)S(1)} %get-tuple-element.12, s32[1024]{0:T(1024)S(1)} %le.3, bf16[1024,256]{1,0:T(8,128)(2,1)S(1)} %reshape.15, bf16[8192,256]{1,0:T(8,128)(2,1)} %get-tuple-element.15), kind=kOutput, calls=%fused_computation.2 | convolution fusion | flops 4328520704 | bytes 38313984 | tf_op jit(solution)/shard_map/cond/branch_1_fun/dot_general | solution.py:30
  183.5 0.0 copy-done
  183.5 14.1 %fusion.3 = f32[1024,256]{1,0:T(8,128)S(1)} fusion(bf16[8192,256]{1,0:T(8,128)(2,1)S(1)} %copy-done, f32[1024,8192]{1,0:T(8,128)} %get-tuple-element.24, f32[1024]{0:T(1024)S(1)} %broadcast_maximum_fusion, s32[8192]{0:T(1024)S(1)} %get-tuple-element.12, s32[1024]{0:T(1024)S(1)} %le.3), kind=kOutput, calls=%fused_computation.5 | convolution fusion | flops 4345298944 | bytes 38838272 | tf_op jit(solution)/shard_map/cond/branch_1_fun/dot_general | solution.py:40
  197.6 15.7 %fusion.2 = f32[1024]{0:T(1024)S(1)} fusion(f32[1024,8192]{1,0:T(8,128)} %get-tuple-element.24, f32[1024]{0:T(1024)S(1)} %broadcast_maximum_fusion, s32[8192]{0:T(1024)S(1)} %get-tuple-element.12, s32[1024]{0:T(1024)S(1)} %le.3), kind=kLoop, calls=%fused_computation.4 | loop fusion | flops 50330624 | bytes 33599488 | tf_op jit(solution)/shard_map/cond/branch_1_fun/reduce_sum | solution.py:39
  213.3 0.2 divide_convert_fusion
  213.5 0.1 convert_element_type.14
  213.7 1.2 fusion.9
  (3 shorter events, 0.0 us)
Async XLA Ops:
  7.2 95.9 %all-gather.3.cloned.1.call-start = ((), (), s32[]{:S(2)}) async-start(), calls=%async_computation | async-start | bytes 4325376 | tf_op jit(solution)/shard_map/all_gather | solution.py:75
  45.9 121.1 %all-gather.5.cloned.1.call-start = ((), (), s32[]{:S(2)}) async-start(), calls=%async_computation.1 | async-start | bytes 4325376 | tf_op jit(solution)/shard_map/all_gather | solution.py:76
  167.4 16.1 %copy-start = (bf16[8192,256]{1,0:T(8,128)(2,1)S(1)}, bf16[8192,256]{1,0:T(8,128)(2,1)}, u32[]{:S(2)}) copy-start(bf16[8192,256]{1,0:T(8,128)(2,1)} %get-tuple-element.16) | copy-start | bytes 12582916 | tf_op jit(solution)/shard_map/cond
Sparse Core Ops, SparseCore 0:
  46.0 56.9 all-gather.2
  106.2 60.8 all-gather.4
where the time goes:
time: 224 us; the launch traced here: 222 us
  waiting for transfers between devices  88.9 us (40%)
  blocking collectives  68 us (30%)
  matrix products  30.2 us (13%)
  other arithmetic  18.1 us (8%)
  between operations  14.7 us (7%)
    all_gather x1, waiting for transfers between devices, on_device(): lax.all_gather(block_values, 'inner', axis=0, tiled=True)  64 us
    all_gather x1, blocking collectives, on_device(): lax.all_gather(shared_keys, 'outer', axis=0, tiled=True)  38.7 us
    all_gather x1, blocking collectives, on_device(): lax.all_gather(shared_values, 'outer', axis=0, tiled=True)  29.3 us
    all_gather x1, waiting for transfers between devices, on_device(): lax.all_gather(block_keys, 'inner', axis=0, tiled=True)  24.9 us
    dot_general x1, matrix products, update(): lax.dot_general(query_rows, key_piece, (((1,), (1,)), ((), ())), preferre...  16 us
    reduce_sum x1, other arithmetic, update(): denominator = jnp.sum(weights, axis=1)  15.7 us
    dot_general x1, matrix products, update(): jnp.dot(weights.astype(jnp.bfloat16), value_piece, preferred_element_type...  14.1 us
  transfers between devices with their start and end apart: 2, of which 2 were waited for; matrix products, arithmetic and copies ran while one was open for 1% of the time, Pallas kernels for 0%

commit v1 on v0

v1 whole, which is shorter than its diff:
```python
import functools
import math

import jax
import jax.numpy as jnp
from jax import lax
from jax.experimental import pallas as pl
from jax.experimental.pallas import tpu as pltpu
from jax.sharding import PartitionSpec as P

MESH = pl.DeviceIdType.MESH
MASKED = -1e30
FLOOR = -1e20
SIDE = 4
DEPTH = 16
SHARD = 16
GROUPS = 8
GROUP_ROWS = 2 * SHARD
BLOCK = DEPTH * SHARD
HALF = SIDE * GROUP_ROWS
LAYER_ROWS = 2 * BLOCK
WIDTH = 256
OFF_OWN, OFF_A1, OFF_A2, OFF_B1, OFF_B2, OFF_USE = 0, 1, 2, 3, 4, 5
TICKS = GROUPS + OFF_USE
TILE = 256


def attention_kernel(
    scale2,
    q1_hbm,
    q2_hbm,
    k_hbm,
    v_hbm,
    o1_ref,
    o2_ref,
    kv,
    q_in,
    q_rows,
    row_max,
    row_sum,
    acc,
    in_sem,
    z_send,
    z_recv,
    a_send,
    a_recv,
    b_send,
    b_recv,
    s_send,
    s_recv,
):
    z = lax.axis_index("outer")
    place = lax.axis_index("inner")
    core = lax.rem(place, 2)
    chip = place // 2
    x = chip // SIDE
    y = lax.rem(chip, SIDE)
    flip = 1 - core
    a = x * flip + y * core
    b = y * flip + x * core

    def shift(value, by, size):
        return lax.rem(value + by + size, size)

    def inner_of(a_place, b_place):
        x_place = a_place * flip + b_place * core
        y_place = b_place * flip + a_place * core
        return (x_place * SIDE + y_place) * 2 + core

    dev_zp = (shift(z, 1, DEPTH), place)
    dev_zm = (shift(z, -1, DEPTH), place)
    dev_ap = (z, inner_of(shift(a, 1, SIDE), b))
    dev_am = (z, inner_of(shift(a, -1, SIDE), b))
    dev_bp = (z, inner_of(a, shift(b, 1, SIDE)))
    dev_bm = (z, inner_of(a, shift(b, -1, SIDE)))
    dev_sib = (z, place + 1 - 2 * core)
    am, ap = shift(a, -1, SIDE), shift(a, 1, SIDE)
    bm, bp, bo = shift(b, -1, SIDE), shift(b, 1, SIDE), shift(b, 2, SIDE)

    first_copies = [
        pltpu.make_async_copy(k_hbm, kv.at[core, 0, b, a, 0, pl.ds(0, SHARD)], in_sem.at[0]),
        pltpu.make_async_copy(v_hbm, kv.at[core, 0, b, a, 1, pl.ds(0, SHARD)], in_sem.at[1]),
    ]
    q_copies = [
        pltpu.make_async_copy(source, q_in.at[n], in_sem.at[2 + n])
        for n, source in enumerate((q1_hbm, q2_hbm))
    ]
    for copy in first_copies + q_copies:
        copy.start()

    barrier = pltpu.get_barrier_semaphore()
    for device in (dev_zp, dev_zm, dev_ap, dev_am, dev_bp, dev_bm, dev_sib):
        pl.semaphore_signal(barrier, inc=1, device_id=device, device_id_type=MESH)
    for copy in first_copies:
        copy.wait()
    pl.semaphore_wait(barrier, 7)

    def remote(src, dst, send, recv, device):
        return pltpu.make_async_remote_copy(
            src_ref=src,
            dst_ref=dst,
            send_sem=send,
            recv_sem=recv,
            device_id=device,
            device_id_type=MESH,
        )

    def shard(g, half):
        return kv.at[core, g, b, a, :, pl.ds(half * SHARD, SHARD)]

    def z_up(s, first=False):
        source = shard(0, 0) if first else shard(jnp.maximum(s - 2, 0), 1)
        return remote(source, shard(s - 1, 1), z_send.at[0, s - 1], z_recv.at[0, s - 1], dev_zm)

    def z_down(s):
        return remote(shard(s - 1, 0), shard(s, 0), z_send.at[1, s - 1], z_recv.at[1, s - 1], dev_zp)

    def own(g, way):
        piece = kv.at[core, g, b, a]
        return remote(piece, piece, a_send.at[way, g], a_recv.at[way, g], (dev_ap, dev_am)[way])

    def a_on(g, way):
        piece = kv.at[core, g, b, (am, ap)[way], way]
        return remote(piece, piece, a_send.at[2 + way, g], a_recv.at[2 + way, g], (dev_ap, dev_am)[way])

    def row_out(g, way):
        piece = kv.at[core, g, b]
        return remote(piece, piece, b_send.at[way, g], b_recv.at[way, g], (dev_bp, dev_bm)[way])

    def b_on(g, way):
        piece = kv.at[core, g, (bm, bp)[way], :, way]
        return remote(piece, piece, b_send.at[2 + way, g], b_recv.at[2 + way, g], (dev_bp, dev_bm)[way])

    def across(g, which):
        piece = kv.at[core, g, (b, bm, bp, bo)[which]]
        return remote(piece, piece, s_send.at[which, g], s_recv.at[which, g], dev_sib)

    z_up(1, True).start()
    z_down(1).start()

    def stage_own(g):
        z_up(g + 1).wait_recv()

        @pl.when(g < GROUPS - 1)
        def _():
            z_up(g + 2).start()
            own(g, 0).start()
            own(g, 1).start()
            z_down(g + 1).wait_recv()

        @pl.when(g == GROUPS - 1)
        def _():
            own(g, 0).start()
            own(g, 1).start()

        @pl.when(g < GROUPS - 2)
        def _():
            z_down(g + 2).start()

    def stage_a1(g):
        for way in (0, 1):
            own(g, way).wait_recv()
            a_on(g, way).start()

    def stage_a2(g):
        for way in (0, 1):
            a_on(g, way).wait_recv()
        for way in (0, 1):
            row_out(g, way).start()
        across(g, 0).start()

    def stage_b1(g):
        for way in (0, 1):
            row_out(g, way).wait_recv()
            b_on(g, way).start()
            across(g, 1 + way).start()

    def stage_b2(g):
        for way in (0, 1):
            b_on(g, way).wait_recv()
        across(g, 3).start()

    def prepare():
        row_max[...] = jnp.full_like(row_max, FLOOR)
        row_sum[...] = jnp.zeros_like(row_sum)
        acc[...] = jnp.zeros_like(acc)
        for n, copy in enumerate(q_copies):
            copy.wait()
            q_rows[n * LAYER_ROWS : (n + 1) * LAYER_ROWS] = q_in[n].reshape(LAYER_ROWS, WIDTH)

    def attend(g, layer, last):
        def keys_of(which):
            pieces = []
            for x_key in range(last + 1):
                pieces.append(kv[0, g, :, x_key, which].reshape(HALF, WIDTH))
                pieces.append(kv[1, g, x_key, :, which].reshape(HALF, WIDTH))
            return jnp.concatenate(pieces, axis=0)

        keys = keys_of(0)
        values = keys_of(1)
        at = lax.broadcasted_iota(jnp.int32, (1, 2 * HALF), 1)
        from_core = at // HALF
        y_key = lax.rem(at // GROUP_ROWS, SIDE)
        z_rel = jnp.where(lax.rem(at // SHARD, 2) == 0, -g, g + 1)
        z_key = lax.rem(z + z_rel + DEPTH, DEPTH)
        key_pos = ((last * SIDE + y_key) * 2 + from_core) * BLOCK + z_key * SHARD + lax.rem(at, SHARD)
        open_width = 2 * HALF * last
        lanes = 2 * (last + 1)
        for tile in range(LAYER_ROWS // TILE):
            here = pl.ds(layer * LAYER_ROWS + tile * TILE, TILE)
            scores = lax.dot_general(
                q_rows[here], keys, (((1,), (1,)), ((), ())), preferred_element_type=jnp.float32
            )
            row = lax.broadcasted_iota(jnp.int32, (TILE, 1), 0) + tile * TILE
            allowed = key_pos <= place * BLOCK + row // 2
            edge = jnp.where(allowed, scores[:, open_width:], MASKED)
            pieces = [scores[:, n * 128 : (n + 1) * 128] for n in range(lanes - 2)]
            pieces += [edge[:, :128], edge[:, 128:]]
            peak = functools.reduce(jnp.maximum, pieces)
            old = row_max[here]
            new = jnp.maximum(old, jnp.max(peak, axis=1, keepdims=True))
            fade = jnp.exp2((old - new) * scale2)
            weights = [jnp.exp2((piece - new) * scale2) for piece in pieces]
            row_max[here] = new
            row_sum[here] = row_sum[here] * fade + functools.reduce(jnp.add, weights)
            rounded = jnp.concatenate([w.astype(jnp.bfloat16) for w in weights], axis=1)
            mixed = jnp.dot(rounded, values, preferred_element_type=jnp.float32)
            acc[here] = acc[here] * jnp.concatenate((fade, fade), axis=1) + mixed

    def use(g, layer):
        for last in range(SIDE):

            @pl.when(x == last)
            def _(last=last):
                attend(g, layer, last)

    def stage_use(g):
        for which in range(4):
            across(g, which).wait_recv()
        use(g, 0)

    def stage_use_second(g):
        use(g, 1)

    def drain(g):
        z_up(g + 1).wait_send()

        @pl.when(g < GROUPS - 1)
        def _():
            z_down(g + 1).wait_send()

        for way in (0, 1):
            own(g, way).wait_send()
            a_on(g, way).wait_send()
            row_out(g, way).wait_send()
            b_on(g, way).wait_send()
        for which in range(4):
            across(g, which).wait_send()

    stages = (
        (OFF_OWN, stage_own),
        (OFF_A1, stage_a1),
        (OFF_A2, stage_a2),
        (OFF_USE, stage_use),
        (OFF_B1, stage_b1),
        (OFF_B2, stage_b2),
        (OFF_USE, stage_use_second),
    )

    @pl.loop(0, TICKS)
    def _(tick):
        for offset, stage in stages:
            g = tick - offset

            @pl.when((g >= 0) & (g < GROUPS))
            def _(stage=stage, g=g):
                stage(g)

        @pl.when(tick == 1)
        def _():
            prepare()

    @pl.loop(0, GROUPS)
    def _(g):
        drain(g)

    for layer, o_ref in enumerate((o1_ref, o2_ref)):
        for part in range(LAYER_ROWS // TILE):
            here = pl.ds(layer * LAYER_ROWS + part * TILE, TILE)
            inverse = 1.0 / jnp.sum(row_sum[here], axis=1, keepdims=True)
            o_ref[part * TILE : (part + 1) * TILE] = (acc[here] * inverse).astype(jnp.bfloat16)


def on_device(queries_first, queries_second, shared_keys, shared_values):
    tokens_here, heads, width = queries_first.shape
    rows = 2 * tokens_here * heads
    scale2 = math.log2(math.e) / math.sqrt(width)
    dma = pltpu.SemaphoreType.DMA
    out = jax.ShapeDtypeStruct((rows // 2, width), jnp.bfloat16)
    vmem = pl.BlockSpec(memory_space=pltpu.VMEM)
    result = pl.pallas_call(
        functools.partial(attention_kernel, scale2),
        out_shape=(out, out),
        in_specs=[pl.BlockSpec(memory_space=pl.ANY)] * 4,
        out_specs=(vmem, vmem),
        scratch_shapes=[
            pltpu.VMEM((2, GROUPS, SIDE, SIDE, 2, GROUP_ROWS, width), jnp.bfloat16),
            pltpu.VMEM((2, tokens_here, heads, width), jnp.bfloat16),
            pltpu.VMEM((rows, width), jnp.bfloat16),
            pltpu.VMEM((rows, 128), jnp.float32),
            pltpu.VMEM((rows, 128), jnp.float32),
            pltpu.VMEM((rows, width), jnp.float32),
            dma((4,)),
            dma((2, GROUPS)),
            dma((2, GROUPS)),
            dma((4, GROUPS)),
            dma((4, GROUPS)),
            dma((4, GROUPS)),
            dma((4, GROUPS)),
            dma((4, GROUPS)),
            dma((4, GROUPS)),
        ],
        compiler_params=pltpu.CompilerParams(
            collective_id=0, has_side_effects=True, vmem_limit_bytes=56 * 1024 * 1024
        ),
        cost_estimate=pl.CostEstimate(
            flops=4 * rows * 8192 * width, bytes_accessed=1 << 20, transcendentals=rows * 8192
        ),
    )(queries_first, queries_second, shared_keys, shared_values)
    return tuple(array.reshape(tokens_here, heads, width) for array in result)


def solution(mesh):
    return jax.shard_map(
        on_device,
        mesh=mesh,
        in_specs=(
            P("inner", "outer", None),
            P("inner", "outer", None),
            P(("inner", "outer"), None),
            P(("inner", "outer"), None),
        ),
        out_specs=(P("inner", "outer", None), P("inner", "outer", None)),
        check_vma=False,
    )
```

time: 224 us -> 63.7 us (0.28)
  waiting for transfers between devices: 88.9 us -> 0 us
  blocking collectives: 68 us -> 0 us
  Pallas kernels: 0 us -> 59.5 us
  matrix products: 30.2 us -> 0 us
  other arithmetic: 18.1 us -> 0 us
  between operations: 14.7 us -> 0.65 us
    all_gather x2 -> x0, waiting for transfers between devices: 88.9 us -> none  [the longest x1 64 us: on_device(): lax.all_gather(block_values, 'inner', axis=0, tiled=True)]
    all_gather x2 -> x0, blocking collectives: 68 us -> none  [the longest x1 38.7 us: on_device(): lax.all_gather(shared_keys, 'outer', axis=0, tiled=True)]
    pallas_call x0 -> x1, Pallas kernels: none -> 59.5 us  [on_device(): pl.pallas_call(functools.partial(attention_kernel, scale2), out_shape=(ou...]
    dot_general x2 -> x0, matrix products: 30.2 us -> none  [the longest x1 16 us: update(): lax.dot_general(query_rows, key_piece, (((1,), (1,)), ((), ())), preferre...]
    reduce_sum x1 -> x0, other arithmetic: 15.7 us -> none  [update(): denominator = jnp.sum(weights, axis=1)]
    reshape x1 -> x2, local copies, waits for them, and re-layouts: 0.12 us -> 2.6 us  [on_device(): return tuple((array.reshape(tokens_here, heads, width) for array in result))]
  transfers between devices with their start and end apart: 2 -> 0, of which waited for: 2 -> 0; matrix products, arithmetic and copies ran while one was open for 1% -> 0% of each run, Pallas kernels for 0% -> 0%
where the time goes in v1:
time: 63.7 us; the launch traced here: 62.8 us
  Pallas kernels  59.5 us (93%)
  local copies, waits for them, and re-layouts  2.6 us (4%)
  between operations  0.65 us (1%)
    pallas_call x1, Pallas kernels, on_device(): pl.pallas_call(functools.partial(attention_kernel, scale2), out_shape=(ou...  59.5 us
    reshape x2, local copies, waits for them, and re-layouts, on_device(): return tuple((array.reshape(tokens_here, heads, width) for array in result))  2.6 us

profile of v1, /device:TPU:6, one launch (start us, length us, event | category | flops | bytes accessed | tf_op | source)
XLA Modules:
  0.0 62.8 jit_solution(12250992970463184920)
XLA Ops:
  0.6 59.5 %shard_map.59 = (bf16[512,256]{1,0:T(8,128)(2,1)}, bf16[512,256]{1,0:T(8,128)(2,1)}) custom-call(bf16[256,2,256]{2,1,0:T(2,128)(2,1)} %q1_hbm.1, bf16[256,2,256]{2,1,0:T(2,128)(2,1)} %q2_hbm.1, bf16[16,256]{1,0:T(8,128)(2,1)} %k_hbm.1, bf16[16,256]{1,0:T(8,128)(2,1)} %v_hbm.1), custom_call_target="tpu_custom_call" | custom-call | flops 8589934592 | bytes 1048576 | tf_op jit(solution)/shard_map/pallas_call | solution.py:301
  60.2 0.0 copy-start
  60.2 1.8 %reshape.10 = bf16[256,2,256]{2,1,0:T(2,128)(2,1)} reshape(bf16[512,256]{1,0:T(8,128)(2,1)} %get-tuple-element.4) | data formatting | bytes 524288 | tf_op jit(solution)/shard_map/reshape | solution.py:330
  62.0 0.0 copy-done
  62.0 0.8 %reshape.11 = bf16[256,2,256]{2,1,0:T(2,128)(2,1)} reshape(bf16[512,256]{1,0:T(8,128)(2,1)S(1)} %copy-done) | data formatting | bytes 524288 | tf_op jit(solution)/shard_map/reshape | solution.py:330
Async XLA Ops:
  60.2 1.8 %copy-start = (bf16[512,256]{1,0:T(8,128)(2,1)S(1)}, bf16[512,256]{1,0:T(8,128)(2,1)}, u32[]{:S(2)}) copy-start(bf16[512,256]{1,0:T(8,128)(2,1)} %get-tuple-element.5) | copy-start | bytes 786436

commit v2 on v1

v2 whole, which is shorter than its diff:
```python
import functools
import math

import jax
import jax.numpy as jnp
from jax import lax
from jax.experimental import pallas as pl
from jax.experimental.pallas import tpu as pltpu
from jax.sharding import PartitionSpec as P

MESH = pl.DeviceIdType.MESH
MASKED = -1e30
FLOOR = -1e20
SIDE = 4
DEPTH = 16
SHARD = 16
GROUP_ROWS = 2 * SHARD
BLOCK = DEPTH * SHARD
HALF = SIDE * GROUP_ROWS
LAYER_ROWS = 2 * BLOCK
ROWS = 2 * LAYER_ROWS
WIDTH = 256
ROUND = ((0, 3), (-3, 1), (5, -5), (7, -7), (-1, 2), (-2, 8))
HOPPED = ((4, -4), (6, -6))
RELATIVE = ROUND + HOPPED
GROUPS = len(ROUND)
HOPS = tuple(
    (which, group, half)
    for which in (0, 1)
    for group in range(GROUPS, len(RELATIVE))
    for half in (0, 1)
)
OFF_OWN, OFF_A1, OFF_A2, OFF_B1, OFF_B2 = 0, 1, 2, 3, 4
TICKS = GROUPS + OFF_B2
TILE = 256
TILES = ROWS // TILE
CHUNK = 64


def place_of(relative):
    for group, members in enumerate(RELATIVE):
        for half, member in enumerate(members):
            if member % DEPTH == relative % DEPTH:
                return group, half
    return None


def attention_kernel(
    scale2,
    q1_hbm,
    q2_hbm,
    k_hbm,
    v_hbm,
    o1_ref,
    o2_ref,
    kv,
    q_in,
    q_cols,
    state,
    acc,
    values_t,
    scores_even,
    scores_odd,
    weights_even,
    weights_odd,
    acc_out,
    acc_in,
    state_in,
    in_sem,
    z_send,
    z_recv,
    a_send,
    a_recv,
    b_send,
    b_recv,
    hop_send,
    hop_recv,
    pair_send,
    pair_recv,
):
    z = lax.axis_index("outer")
    place = lax.axis_index("inner")
    core = lax.rem(place, 2)
    chip = place // 2
    x = chip // SIDE
    y = lax.rem(chip, SIDE)
    flip = 1 - core
    a = x * flip + y * core
    b = y * flip + x * core

    def shift(value, by, size):
        return lax.rem(value + by + size, size)

    def inner_of(a_place, b_place):
        x_place = a_place * flip + b_place * core
        y_place = b_place * flip + a_place * core
        return (x_place * SIDE + y_place) * 2 + core

    dev_zp = (shift(z, 1, DEPTH), place)
    dev_zm = (shift(z, -1, DEPTH), place)
    dev_ap = (z, inner_of(shift(a, 1, SIDE), b))
    dev_am = (z, inner_of(shift(a, -1, SIDE), b))
    dev_bp = (z, inner_of(a, shift(b, 1, SIDE)))
    dev_bm = (z, inner_of(a, shift(b, -1, SIDE)))
    dev_sib = (z, place + 1 - 2 * core)
    am, ap = shift(a, -1, SIDE), shift(a, 1, SIDE)
    bm, bp = shift(b, -1, SIDE), shift(b, 1, SIDE)

    first_copies = [
        pltpu.make_async_copy(k_hbm, kv.at[core, 0, b, a, 0, pl.ds(0, SHARD)], in_sem.at[0]),
        pltpu.make_async_copy(v_hbm, kv.at[core, 0, b, a, 1, pl.ds(0, SHARD)], in_sem.at[1]),
    ]
    q_copies = [
        pltpu.make_async_copy(source, q_in.at[n], in_sem.at[2 + n])
        for n, source in enumerate((q1_hbm, q2_hbm))
    ]
    for copy in first_copies + q_copies:
        copy.start()

    far = [member for pair in ROUND for member in pair if member]
    barrier = pltpu.get_barrier_semaphore()
    for device in (dev_ap, dev_am, dev_bp, dev_bm, dev_sib):
        pl.semaphore_signal(barrier, inc=1, device_id=device, device_id_type=MESH)
    for member in far:
        device = (shift(z, -member, DEPTH), place)
        pl.semaphore_signal(barrier, inc=1, device_id=device, device_id_type=MESH)
    for copy in first_copies:
        copy.wait()
    pl.semaphore_wait(barrier, 5 + len(far))

    def remote(src, dst, send, recv, device):
        return pltpu.make_async_remote_copy(
            src_ref=src,
            dst_ref=dst,
            send_sem=send,
            recv_sem=recv,
            device_id=device,
            device_id_type=MESH,
        )

    def shard(g, half):
        return kv.at[core, g, b, a, :, pl.ds(half * SHARD, SHARD)]

    def z_out(g, half, device):
        return remote(shard(0, 0), shard(g, half), z_send.at[g, half], z_recv.at[g, half], device)

    def own(g, way):
        piece = kv.at[core, g, b, a]
        return remote(piece, piece, a_send.at[way, g], a_recv.at[way, g], (dev_ap, dev_am)[way])

    def a_on(g, way):
        piece = kv.at[core, g, b, (am, ap)[way], way]
        return remote(piece, piece, a_send.at[2 + way, g], a_recv.at[2 + way, g], (dev_ap, dev_am)[way])

    def row_out(g, way):
        piece = kv.at[core, g, b]
        return remote(piece, piece, b_send.at[way, g], b_recv.at[way, g], (dev_bp, dev_bm)[way])

    def b_on(g, way):
        piece = kv.at[core, g, (bm, bp)[way], :, way]
        return remote(piece, piece, b_send.at[2 + way, g], b_recv.at[2 + way, g], (dev_bp, dev_bm)[way])

    def hop(n):
        which, group, half = HOPS[n]
        member = RELATIVE[group][half]
        source_group, source_half = place_of(member - 1 if which == 0 else member + 1)
        source = kv.at[core, source_group, :, :, which, pl.ds(source_half * SHARD, SHARD)]
        target = kv.at[core, group, :, :, which, pl.ds(half * SHARD, SHARD)]
        device = dev_zm if which == 0 else dev_zp
        return source_group, remote(source, target, hop_send.at[n], hop_recv.at[n], device)

    mine, theirs = pl.ds(0, TILES), pl.ds(TILES, TILES)
    q_across = remote(q_cols.at[mine], q_cols.at[theirs], pair_send.at[0], pair_recv.at[0], dev_sib)
    acc_across = remote(acc_out, acc_in, pair_send.at[1], pair_recv.at[1], dev_sib)
    state_across = remote(state.at[theirs], state_in, pair_send.at[2], pair_recv.at[2], dev_sib)

    for member in far:
        z_out(*place_of(member), (shift(z, -member, DEPTH), place)).start()

    def prepare(step):
        if step < 2:
            q_copies[step].wait()
            for part in range(TILES // 2):
                tokens = TILE // 2
                rows = q_in[step, part * tokens : (part + 1) * tokens].reshape(TILE, WIDTH)
                q_cols[step * (TILES // 2) + part] = rows.T
            if step == 1:
                q_across.start()
        else:
            start = (step - 2) * TILES
            acc[start : start + TILES] = jnp.zeros((TILES, WIDTH, TILE), jnp.float32)
            state[start : start + TILES, 0:1] = jnp.full((TILES, 1, TILE), FLOOR, jnp.float32)
            state[start : start + TILES, 1:2] = jnp.zeros((TILES, 1, TILE), jnp.float32)

    def stage_own(g):
        @pl.when(g > 0)
        def _():
            z_out(g, 0, dev_zp).wait_recv()

        z_out(g, 1, dev_zp).wait_recv()
        own(g, 0).start()
        own(g, 1).start()

    def stage_a1(g):
        for way in (0, 1):
            own(g, way).wait_recv()
            a_on(g, way).start()

    def stage_a2(g):
        for way in (0, 1):
            a_on(g, way).wait_recv()
        for way in (0, 1):
            row_out(g, way).start()

    def stage_b1(g):
        for way in (0, 1):
            row_out(g, way).wait_recv()
            b_on(g, way).start()

    def stage_b2(g):
        for way in (0, 1):
            b_on(g, way).wait_recv()
        for n in range(len(HOPS)):
            source_group, copy = hop(n)

            @pl.when(g == source_group)
            def _(copy=copy):
                copy.start()

    def select(g, half):
        value = jnp.int32(0)
        for group, members in enumerate(RELATIVE):
            value = jnp.where(g == group, members[half], value)
        return value

    def attend(g, step, token_block, side, last):
        def keys_of(which):
            pieces = []
            for x_key in range(last + 1):
                piece = kv[0, g, :, x_key, which] if side == 0 else kv[1, g, x_key, :, which]
                pieces.append(piece.reshape(HALF, WIDTH))
            return jnp.concatenate(pieces, axis=0)

        open_keys = last * HALF
        all_keys = open_keys + HALF

        @pl.when(step == 0)
        def _():
            values_t[g, :, :all_keys] = keys_of(1).T

        at = lax.broadcasted_iota(jnp.int32, (HALF, 1), 0)
        y_key = at // GROUP_ROWS
        z_rel = jnp.where(lax.rem(at // SHARD, 2) == 0, select(g, 0), select(g, 1))
        z_key = lax.rem(z + z_rel + DEPTH, DEPTH)
        key_pos = ((last * SIDE + y_key) * 2 + side) * BLOCK + z_key * SHARD + lax.rem(at, SHARD)
        limit = token_block * BLOCK + lax.broadcasted_iota(jnp.int32, (1, TILE), 1) // 2

        base = (1 - step) * TILES
        score_refs = (scores_even, scores_odd)
        weight_refs = (weights_even, weights_odd)
        before = state[pl.ds(base, TILES)]
        maxima, totals, fades = [], [], []

        def score_tile(n):
            score_refs[n % 2][:all_keys] = jnp.dot(
                keys_of(0), q_cols[base + n], preferred_element_type=jnp.float32
            )

        def soften_tile(n):
            source, target = score_refs[n % 2], weight_refs[n % 2]
            allowed = key_pos <= limit + (n % 2) * (TILE // 2)

            def chunk(first):
                scores = source[first : first + CHUNK]
                if first >= open_keys:
                    row = first - open_keys
                    scores = jnp.where(allowed[row : row + CHUNK], scores, MASKED)
                return scores

            def fold(op, values):
                return functools.reduce(op, [values[i : i + 8] for i in range(0, CHUNK, 8)])

            peak = functools.reduce(
                jnp.maximum, [fold(jnp.maximum, chunk(first)) for first in range(0, all_keys, CHUNK)]
            )
            old = before[n, 0:1]
            new = jnp.maximum(old, jnp.max(peak, axis=0, keepdims=True))
            total = jnp.zeros((8, TILE), jnp.float32)
            for first in range(0, all_keys, CHUNK):
                weights = jnp.exp2((chunk(first) - new) * scale2)
                total = total + fold(jnp.add, weights)
                target[first : first + CHUNK] = weights.astype(jnp.bfloat16)
            fade = jnp.exp2((old - new) * scale2)
            fades.append(fade)
            maxima.append(new)
            totals.append(before[n, 1:2] * fade + jnp.sum(total, axis=0, keepdims=True))

        def mix_tile(n):
            mixed = jnp.dot(
                values_t[g, :, :all_keys],
                weight_refs[n % 2][:all_keys],
                preferred_element_type=jnp.float32,
            )
            acc[base + n] = acc[base + n] * fades[n] + mixed

        score_tile(0)
        for n in range(TILES):
            if n + 1 < TILES:
                score_tile(n + 1)
            if n:
                mix_tile(n - 1)
            soften_tile(n)
        mix_tile(TILES - 1)
        for n in range(TILES):
            state[base + n, 0:1] = maxima[n]
            state[base + n, 1:2] = totals[n]

    def use(g, step):
        token_block = place + (1 - step) * (1 - 2 * core)
        for side in (0, 1):
            for last in range(SIDE):

                @pl.when((core == side) & (x == last))
                def _(side=side, last=last):
                    attend(g, step, token_block, side, last)

    def hand_over():
        state_across.start()
        for tile in range(TILES):
            acc_out[tile] = acc[TILES + tile].astype(jnp.bfloat16)
        acc_across.start()

    stages = (
        (OFF_OWN, stage_own),
        (OFF_A1, stage_a1),
        (OFF_A2, stage_a2),
        (OFF_B1, stage_b1),
        (OFF_B2, stage_b2),
    )
    hop_tick = OFF_B2 + 3

    @pl.loop(0, TICKS)
    def _(tick):
        for offset, stage in stages:
            g = tick - offset

            @pl.when((g >= 0) & (g < GROUPS))
            def _(stage=stage, g=g):
                stage(g)

        for step in range(OFF_B2):

            @pl.when(tick == step)
            def _(step=step):
                prepare(step)

        @pl.when(tick == OFF_B2)
        def _():
            q_across.wait_recv()

        hopped = (tick >= hop_tick) & (tick < hop_tick + len(HOPPED))
        closing = tick == TICKS - 1
        first = tick - OFF_B2
        hop_group = tick - hop_tick + GROUPS
        count = jnp.where(
            first < 0, 0, jnp.where(hopped, 4, jnp.where(closing, 3, jnp.where(first == 0, 1, 2)))
        )

        @pl.loop(0, count)
        def _(item):
            for n, (_, group, _) in enumerate(HOPS):

                @pl.when((item == 2) & hopped & (hop_group == group))
                def _(n=n):
                    hop(n)[1].wait_recv()

            @pl.when(closing & (item == 1))
            def _():
                hand_over()

            group = jnp.where(
                item == 0, first, jnp.where(item == 1, first - 1, jnp.where(closing, first, hop_group))
            )
            use(group, jnp.where(item == 2, jnp.where(closing, 1, 0), jnp.minimum(item, 1)))

    for member in far:
        z_out(*place_of(member), dev_zp).wait_send()
    for n in range(len(HOPS)):
        hop(n)[1].wait_send()
    q_across.wait_send()

    @pl.loop(0, GROUPS)
    def _(g):
        for way in (0, 1):
            own(g, way).wait_send()
            a_on(g, way).wait_send()
            row_out(g, way).wait_send()
            b_on(g, way).wait_send()

    state_across.wait()
    acc_across.wait()
    for layer, o_ref in enumerate((o1_ref, o2_ref)):
        for part in range(TILES // 2):
            tile = layer * (TILES // 2) + part
            here, there = state[tile, 0:1], state_in[tile, 0:1]
            peak = jnp.maximum(here, there)
            keep = jnp.exp2((here - peak) * scale2)
            add = jnp.exp2((there - peak) * scale2)
            inverse = 1.0 / (state[tile, 1:2] * keep + state_in[tile, 1:2] * add)
            result = acc[tile] * (keep * inverse) + acc_in[tile].astype(jnp.float32) * (add * inverse)
            o_ref[part * TILE : (part + 1) * TILE] = result.T.astype(jnp.bfloat16)


def on_device(queries_first, queries_second, shared_keys, shared_values):
    tokens_here, heads, width = queries_first.shape
    rows = 2 * tokens_here * heads
    scale2 = math.log2(math.e) / math.sqrt(width)
    dma = pltpu.SemaphoreType.DMA
    out = jax.ShapeDtypeStruct((rows // 2, width), jnp.bfloat16)
    vmem = pl.BlockSpec(memory_space=pltpu.VMEM)
    result = pl.pallas_call(
        functools.partial(attention_kernel, scale2),
        out_shape=(out, out),
        in_specs=[pl.BlockSpec(memory_space=pl.ANY)] * 4,
        out_specs=(vmem, vmem),
        scratch_shapes=[
            pltpu.VMEM((2, len(RELATIVE), SIDE, SIDE, 2, GROUP_ROWS, width), jnp.bfloat16),
            pltpu.VMEM((2, tokens_here, heads, width), jnp.bfloat16),
            pltpu.VMEM((2 * TILES, width, TILE), jnp.bfloat16),
            pltpu.VMEM((2 * TILES, 2, TILE), jnp.float32),
            pltpu.VMEM((2 * TILES, width, TILE), jnp.float32),
            pltpu.VMEM((len(RELATIVE), width, SIDE * HALF), jnp.bfloat16),
            pltpu.VMEM((SIDE * HALF, TILE), jnp.float32),
            pltpu.VMEM((SIDE * HALF, TILE), jnp.float32),
            pltpu.VMEM((SIDE * HALF, TILE), jnp.bfloat16),
            pltpu.VMEM((SIDE * HALF, TILE), jnp.bfloat16),
            pltpu.VMEM((TILES, width, TILE), jnp.bfloat16),
            pltpu.VMEM((TILES, width, TILE), jnp.bfloat16),
            pltpu.VMEM((TILES, 2, TILE), jnp.float32),
            dma((4,)),
            dma((GROUPS, 2)),
            dma((GROUPS, 2)),
            dma((4, GROUPS)),
            dma((4, GROUPS)),
            dma((4, GROUPS)),
            dma((4, GROUPS)),
            dma((len(HOPS),)),
            dma((len(HOPS),)),
            dma((3,)),
            dma((3,)),
        ],
        compiler_params=pltpu.CompilerParams(
            collective_id=0, has_side_effects=True, vmem_limit_bytes=56 * 1024 * 1024
        ),
        cost_estimate=pl.CostEstimate(
            flops=4 * rows * 8192 * width, bytes_accessed=1 << 20, transcendentals=rows * 8192
        ),
    )(queries_first, queries_second, shared_keys, shared_values)
    return tuple(array.reshape(tokens_here, heads, width) for array in result)


def solution(mesh):
    return jax.shard_map(
        on_device,
        mesh=mesh,
        in_specs=(
            P("inner", "outer", None),
            P("inner", "outer", None),
            P(("inner", "outer"), None),
            P(("inner", "outer"), None),
        ),
        out_specs=(P("inner", "outer", None), P("inner", "outer", None)),
        check_vma=False,
    )
```

time: 63.7 us -> 66.9 us (1.050); the launches traced: 62.8 us -> 66.8 us
  Pallas kernels: 59.5 us -> 63.5 us
    pallas_call x1, Pallas kernels: 59.5 us -> 63.5 us  [on_device(): pl.pallas_call(functools.partial(attention_kernel, scale2), out_shape=(ou...]
where the time goes in v2:
time: 66.9 us; the launch traced here: 66.8 us
  Pallas kernels  63.5 us (95%)
  local copies, waits for them, and re-layouts  2.6 us (4%)
    pallas_call x1, Pallas kernels, on_device(): pl.pallas_call(functools.partial(attention_kernel, scale2), out_shape=(ou...  63.5 us
    reshape x2, local copies, waits for them, and re-layouts, on_device(): return tuple((array.reshape(tokens_here, heads, width) for array in result))  2.6 us

profile of v2, /device:TPU:6, one launch (start us, length us, event | category | flops | bytes accessed | tf_op | source)
XLA Modules:
  0.0 66.8 jit_solution(9009590828740079710)
XLA Ops:
  0.6 63.5 %shard_map.59 = (bf16[512,256]{1,0:T(8,128)(2,1)}, bf16[512,256]{1,0:T(8,128)(2,1)}) custom-call(bf16[256,2,256]{2,1,0:T(2,128)(2,1)} %q1_hbm.1, bf16[256,2,256]{2,1,0:T(2,128)(2,1)} %q2_hbm.1, bf16[16,256]{1,0:T(8,128)(2,1)} %k_hbm.1, bf16[16,256]{1,0:T(8,128)(2,1)} %v_hbm.1), custom_call_target="tpu_custom_call" | custom-call | flops 8589934592 | bytes 1048576 | tf_op jit(solution)/shard_map/pallas_call | solution.py:421
  64.2 0.0 copy-start
  64.2 1.8 %reshape.10 = bf16[256,2,256]{2,1,0:T(2,128)(2,1)} reshape(bf16[512,256]{1,0:T(8,128)(2,1)} %get-tuple-element.4) | data formatting | bytes 524288 | tf_op jit(solution)/shard_map/reshape | solution.py:459
  66.0 0.0 copy-done
  66.0 0.8 %reshape.11 = bf16[256,2,256]{2,1,0:T(2,128)(2,1)} reshape(bf16[512,256]{1,0:T(8,128)(2,1)S(1)} %copy-done) | data formatting | bytes 524288 | tf_op jit(solution)/shard_map/reshape | solution.py:459
Async XLA Ops:
  64.2 1.8 %copy-start = (bf16[512,256]{1,0:T(8,128)(2,1)S(1)}, bf16[512,256]{1,0:T(8,128)(2,1)}, u32[]{:S(2)}) copy-start(bf16[512,256]{1,0:T(8,128)(2,1)} %get-tuple-element.5) | copy-start | bytes 786436

commit v3 on v1

--- a/solution.py
+++ b/solution.py
@@ -14,15 +14,33 @@
 SIDE = 4
 DEPTH = 16
 SHARD = 16
-GROUPS = 8
 GROUP_ROWS = 2 * SHARD
 BLOCK = DEPTH * SHARD
 HALF = SIDE * GROUP_ROWS
 LAYER_ROWS = 2 * BLOCK
 WIDTH = 256
+ROUND = ((0, 1), (3, -3), (5, -5), (7, -7), (-1, 2), (-2, 8))
+HOPPED = ((4, -4), (6, -6))
+RELATIVE = ROUND + HOPPED
+GROUPS = len(ROUND)
+HOPS = tuple(
+    (which, group, half)
+    for group in range(GROUPS, len(RELATIVE))
+    for which in (0, 1)
+    for half in (0, 1)
+)
+ONWARD = ((1, -2, 3), (-1, 2, -3), (3, -2, 5), (-3, 2, -5), (5, -2, 7), (-5, 2, -7), (7, -1, 8))
 OFF_OWN, OFF_A1, OFF_A2, OFF_B1, OFF_B2, OFF_USE = 0, 1, 2, 3, 4, 5
 TICKS = GROUPS + OFF_USE
 TILE = 256
+
+
+def place_of(relative):
+    for group, members in enumerate(RELATIVE):
+        for half, member in enumerate(members):
+            if member % DEPTH == relative % DEPTH:
+                return group, half
+    return None
 
 
 def attention_kernel(
@@ -48,6 +66,8 @@
     b_recv,
     s_send,
     s_recv,
+    hop_send,
+    hop_recv,
 ):
     z = lax.axis_index("outer")
     place = lax.axis_index("inner")
@@ -67,8 +87,7 @@
         y_place = b_place * flip + a_place * core
         return (x_place * SIDE + y_place) * 2 + core
 
-    dev_zp = (shift(z, 1, DEPTH), place)
-    dev_zm = (shift(z, -1, DEPTH), place)
+    along_z = {by: (shift(z, by, DEPTH), place) for by in (-2, -1, 1, 2)}
     dev_ap = (z, inner_of(shift(a, 1, SIDE), b))
     dev_am = (z, inner_of(shift(a, -1, SIDE), b))
     dev_bp = (z, inner_of(a, shift(b, 1, SIDE)))
@@ -89,11 +108,11 @@
         copy.start()
 
     barrier = pltpu.get_barrier_semaphore()
-    for device in (dev_zp, dev_zm, dev_ap, dev_am, dev_bp, dev_bm, dev_sib):
+    for device in (*along_z.values(), dev_ap, dev_am, dev_bp, dev_bm, dev_sib):
         pl.semaphore_signal(barrier, inc=1, device_id=device, device_id_type=MESH)
     for copy in first_copies:
         copy.wait()
-    pl.semaphore_wait(barrier, 7)
+    pl.semaphore_wait(barrier, 9)
 
     def remote(src, dst, send, recv, device):
         return pltpu.make_async_remote_copy(
@@ -108,12 +127,16 @@
     def shard(g, half):
         return kv.at[core, g, b, a, :, pl.ds(half * SHARD, SHARD)]
 
-    def z_up(s, first=False):
-        source = shard(0, 0) if first else shard(jnp.maximum(s - 2, 0), 1)
-        return remote(source, shard(s - 1, 1), z_send.at[0, s - 1], z_recv.at[0, s - 1], dev_zm)
-
-    def z_down(s):
-        return remote(shard(s - 1, 0), shard(s, 0), z_send.at[1, s - 1], z_recv.at[1, s - 1], dev_zp)
+    def z_move(source, by, target):
+        g, half = place_of(target)
+        return remote(
+            shard(*place_of(source)), shard(g, half), z_send.at[g, half], z_recv.at[g, half], along_z[by]
+        )
+
+    starts = [z_move(0, -by, by) for by in (1, -1, 2, -2)]
+    onward = {source: z_move(source, by, target) for source, by, target in ONWARD}
+    arrivals = {target: move for move, target in zip(starts, (1, -1, 2, -2))}
+    arrivals.update({target: onward[source] for source, _, target in ONWARD})
 
     def own(g, way):
         piece = kv.at[core, g, b, a]
@@ -135,27 +158,36 @@
         piece = kv.at[core, g, (b, bm, bp, bo)[which]]
         return remote(piece, piece, s_send.at[which, g], s_recv.at[which, g], dev_sib)
 
-    z_up(1, True).start()
-    z_down(1).start()
+    def hop(n):
+        which, group, half = HOPS[n]
+        member = RELATIVE[group][half]
+        source_group, source_half = place_of(member - 1 if which == 0 else member + 1)
+        source = kv.at[core, source_group, :, :, which, pl.ds(source_half * SHARD, SHARD)]
+        target = kv.at[core, group, :, :, which, pl.ds(half * SHARD, SHARD)]
+        device = along_z[-1 if which == 0 else 1]
+        return source_group, remote(source, target, hop_send.at[n], hop_recv.at[n], device)
+
+    def across_hopped(g):
+        piece = kv.at[core, g]
+        n = g - GROUPS
+        return remote(piece, piece, s_send.at[4, n], s_recv.at[4, n], dev_sib)
+
+    for move in starts:
+        move.start()
 
     def stage_own(g):
-        z_up(g + 1).wait_recv()
-
-        @pl.when(g < GROUPS - 1)
-        def _():
-            z_up(g + 2).start()
-            own(g, 0).start()
-            own(g, 1).start()
-            z_down(g + 1).wait_recv()
-
-        @pl.when(g == GROUPS - 1)
-        def _():
-            own(g, 0).start()
-            own(g, 1).start()
-
-        @pl.when(g < GROUPS - 2)
-        def _():
-            z_down(g + 2).start()
+        for group, members in enumerate(ROUND):
+
+            @pl.when(g == group)
+            def _(group=group, members=members):
+                waited = (1, -1) if group == 0 else tuple(m for m in members if m != -1)
+                for member in waited:
+                    arrivals[member].wait_recv()
+                    if member in onward:
+                        onward[member].start()
+
+        own(g, 0).start()
+        own(g, 1).start()
 
     def stage_a1(g):
         for way in (0, 1):
@@ -179,14 +211,37 @@
         for way in (0, 1):
             b_on(g, way).wait_recv()
         across(g, 3).start()
-
-    def prepare():
-        row_max[...] = jnp.full_like(row_max, FLOOR)
-        row_sum[...] = jnp.zeros_like(row_sum)
-        acc[...] = jnp.zeros_like(acc)
-        for n, copy in enumerate(q_copies):
-            copy.wait()
-            q_rows[n * LAYER_ROWS : (n + 1) * LAYER_ROWS] = q_in[n].reshape(LAYER_ROWS, WIDTH)
+        for n in range(len(HOPS)):
+            source_group, copy = hop(n)
+
+            @pl.when(g == source_group)
+            def _(copy=copy):
+                copy.start()
+
+    def stage_hopped(g):
+        for n, (_, group, _) in enumerate(HOPS):
+
+            @pl.when(g == group)
+            def _(n=n):
+                hop(n)[1].wait_recv()
+
+        across_hopped(g).start()
+
+    def select(g, half):
+        value = jnp.int32(0)
+        for group, members in enumerate(RELATIVE):
+            value = jnp.where(g == group, members[half], value)
+        return value
+
+    def prepare(step):
+        if step < 2:
+            q_copies[step].wait()
+            q_rows[step * LAYER_ROWS : (step + 1) * LAYER_ROWS] = q_in[step].reshape(LAYER_ROWS, WIDTH)
+        elif step == 2:
+            row_max[...] = jnp.full_like(row_max, FLOOR)
+            row_sum[...] = jnp.zeros_like(row_sum)
+        else:
+            acc[...] = jnp.zeros_like(acc)
 
     def attend(g, layer, last):
         def keys_of(which):
@@ -201,13 +256,14 @@
         at = lax.broadcasted_iota(jnp.int32, (1, 2 * HALF), 1)
         from_core = at // HALF
         y_key = lax.rem(at // GROUP_ROWS, SIDE)
-        z_rel = jnp.where(lax.rem(at // SHARD, 2) == 0, -g, g + 1)
+        z_rel = jnp.where(lax.rem(at // SHARD, 2) == 0, select(g, 0), select(g, 1))
         z_key = lax.rem(z + z_rel + DEPTH, DEPTH)
         key_pos = ((last * SIDE + y_key) * 2 + from_core) * BLOCK + z_key * SHARD + lax.rem(at, SHARD)
         open_width = 2 * HALF * last
         lanes = 2 * (last + 1)
+        start = layer * LAYER_ROWS
         for tile in range(LAYER_ROWS // TILE):
-            here = pl.ds(layer * LAYER_ROWS + tile * TILE, TILE)
+            here = pl.ds(pl.multiple_of(start + tile * TILE, TILE), TILE)
             scores = lax.dot_general(
                 q_rows[here], keys, (((1,), (1,)), ((), ())), preferred_element_type=jnp.float32
             )
@@ -239,16 +295,7 @@
             across(g, which).wait_recv()
         use(g, 0)
 
-    def stage_use_second(g):
-        use(g, 1)
-
     def drain(g):
-        z_up(g + 1).wait_send()
-
-        @pl.when(g < GROUPS - 1)
-        def _():
-            z_down(g + 1).wait_send()
-
         for way in (0, 1):
             own(g, way).wait_send()
             a_on(g, way).wait_send()
@@ -264,8 +311,8 @@
         (OFF_USE, stage_use),
         (OFF_B1, stage_b1),
         (OFF_B2, stage_b2),
-        (OFF_USE, stage_use_second),
     )
+    hop_tick = TICKS - len(HOPPED)
 
     @pl.loop(0, TICKS)
     def _(tick):
@@ -276,9 +323,36 @@
             def _(stage=stage, g=g):
                 stage(g)
 
-        @pl.when(tick == 1)
+        for step in range(4):
+
+            @pl.when(tick == step)
+            def _(step=step):
+                prepare(step)
+
+        hopped = tick >= hop_tick
+        hop_group = jnp.where(hopped, tick - hop_tick + GROUPS, GROUPS)
+
+        @pl.when(hopped)
         def _():
-            prepare()
+            stage_hopped(hop_group)
+
+        @pl.loop(0, jnp.where(hopped, 3, jnp.where(tick >= OFF_USE, 1, 0)))
+        def _(item):
+            @pl.when(item == 1)
+            def _():
+                across_hopped(hop_group).wait_recv()
+                use(hop_group, 0)
+
+            @pl.when(item != 1)
+            def _():
+                use(jnp.where(item == 0, tick - OFF_USE, hop_group), 1)
+
+    for move in arrivals.values():
+        move.wait_send()
+    for n in range(len(HOPS)):
+        hop(n)[1].wait_send()
+    for g in range(GROUPS, len(RELATIVE)):
+        across_hopped(g).wait_send()
 
     @pl.loop(0, GROUPS)
     def _(g):
@@ -304,21 +378,23 @@
         in_specs=[pl.BlockSpec(memory_space=pl.ANY)] * 4,
         out_specs=(vmem, vmem),
         scratch_shapes=[
-            pltpu.VMEM((2, GROUPS, SIDE, SIDE, 2, GROUP_ROWS, width), jnp.bfloat16),
+            pltpu.VMEM((2, len(RELATIVE), SIDE, SIDE, 2, GROUP_ROWS, width), jnp.bfloat16),
             pltpu.VMEM((2, tokens_here, heads, width), jnp.bfloat16),
             pltpu.VMEM((rows, width), jnp.bfloat16),
             pltpu.VMEM((rows, 128), jnp.float32),
             pltpu.VMEM((rows, 128), jnp.float32),
             pltpu.VMEM((rows, width), jnp.float32),
             dma((4,)),
-            dma((2, GROUPS)),
-            dma((2, GROUPS)),
+            dma((GROUPS, 2)),
+            dma((GROUPS, 2)),
             dma((4, GROUPS)),
             dma((4, GROUPS)),
             dma((4, GROUPS)),
             dma((4, GROUPS)),
-            dma((4, GROUPS)),
-            dma((4, GROUPS)),
+            dma((5, GROUPS)),
+            dma((5, GROUPS)),
+            dma((len(HOPS),)),
+            dma((len(HOPS),)),
         ],
         compiler_params=pltpu.CompilerParams(
             collective_id=0, has_side_effects=True, vmem_limit_bytes=56 * 1024 * 1024

time: 63.7 us -> 64.3 us (level); the launches traced: 62.8 us -> 64.1 us
  Pallas kernels: 59.5 us -> 60.9 us
    pallas_call x1, Pallas kernels: 59.5 us -> 60.9 us  [on_device(): pl.pallas_call(functools.partial(attention_kernel, scale2), out_shape=(ou...]
where the time goes in v3:
time: 64.3 us; the launch traced here: 64.1 us
  Pallas kernels  60.9 us (95%)
  local copies, waits for them, and re-layouts  2.6 us (4%)
  between operations  0.65 us (1%)
    pallas_call x1, Pallas kernels, on_device(): pl.pallas_call(functools.partial(attention_kernel, scale2), out_shape=(ou...  60.9 us
    reshape x2, local copies, waits for them, and re-layouts, on_device(): return tuple((array.reshape(tokens_here, heads, width) for array in result))  2.6 us

profile of v3, /device:TPU:6, one launch (start us, length us, event | category | flops | bytes accessed | tf_op | source)
XLA Modules:
  0.0 64.1 jit_solution(10577027305069787946)
XLA Ops:
  0.6 60.9 %shard_map.59 = (bf16[512,256]{1,0:T(8,128)(2,1)}, bf16[512,256]{1,0:T(8,128)(2,1)}) custom-call(bf16[256,2,256]{2,1,0:T(2,128)(2,1)} %q1_hbm.1, bf16[256,2,256]{2,1,0:T(2,128)(2,1)} %q2_hbm.1, bf16[16,256]{1,0:T(8,128)(2,1)} %k_hbm.1, bf16[16,256]{1,0:T(8,128)(2,1)} %v_hbm.1), custom_call_target="tpu_custom_call" | custom-call | flops 8589934592 | bytes 1048576 | tf_op jit(solution)/shard_map/pallas_call | solution.py:375
  61.5 0.0 copy-start
  61.5 1.8 %reshape.10 = bf16[256,2,256]{2,1,0:T(2,128)(2,1)} reshape(bf16[512,256]{1,0:T(8,128)(2,1)} %get-tuple-element.4) | data formatting | bytes 524288 | tf_op jit(solution)/shard_map/reshape | solution.py:406
  63.3 0.0 copy-done
  63.3 0.8 %reshape.11 = bf16[256,2,256]{2,1,0:T(2,128)(2,1)} reshape(bf16[512,256]{1,0:T(8,128)(2,1)S(1)} %copy-done) | data formatting | bytes 524288 | tf_op jit(solution)/shard_map/reshape | solution.py:406
Async XLA Ops:
  61.5 1.8 %copy-start = (bf16[512,256]{1,0:T(8,128)(2,1)S(1)}, bf16[512,256]{1,0:T(8,128)(2,1)}, u32[]{:S(2)}) copy-start(bf16[512,256]{1,0:T(8,128)(2,1)} %get-tuple-element.5) | copy-start | bytes 786436

commit v4 on v3

--- a/solution.py
+++ b/solution.py
@@ -18,6 +18,7 @@
 BLOCK = DEPTH * SHARD
 HALF = SIDE * GROUP_ROWS
 LAYER_ROWS = 2 * BLOCK
+ROWS = 2 * LAYER_ROWS
 WIDTH = 256
 ROUND = ((0, 1), (3, -3), (5, -5), (7, -7), (-1, 2), (-2, 8))
 HOPPED = ((4, -4), (6, -6))
@@ -30,8 +31,28 @@
     for half in (0, 1)
 )
 ONWARD = ((1, -2, 3), (-1, 2, -3), (3, -2, 5), (-3, 2, -5), (5, -2, 7), (-5, 2, -7), (7, -1, 8))
-OFF_OWN, OFF_A1, OFF_A2, OFF_B1, OFF_B2, OFF_USE = 0, 1, 2, 3, 4, 5
-TICKS = GROUPS + OFF_USE
+OFF_OWN, OFF_A1, OFF_A2, OFF_B1, OFF_B2 = 0, 1, 2, 3, 4
+TICKS = GROUPS + OFF_B2
+MINE, SIBLING = 0, 1
+ITEMS = (
+    (4, 0, SIBLING),
+    (5, 1, SIBLING),
+    (5, 0, MINE),
+    (6, 2, SIBLING),
+    (6, 1, MINE),
+    (7, 3, SIBLING),
+    (7, 2, MINE),
+    (8, 4, SIBLING),
+    (8, 3, MINE),
+    (8, 6, SIBLING),
+    (8, 6, MINE),
+    (9, 5, SIBLING),
+    (9, 7, SIBLING),
+    (9, 4, MINE),
+    (9, 5, MINE),
+    (9, 7, MINE),
+)
+HAND_OVER = 13
 TILE = 256
 
 
@@ -57,6 +78,10 @@
     row_max,
     row_sum,
     acc,
+    acc_out,
+    acc_in,
+    stat_out,
+    stat_in,
     in_sem,
     z_send,
     z_recv,
@@ -64,8 +89,8 @@
     a_recv,
     b_send,
     b_recv,
-    s_send,
-    s_recv,
+    pair_send,
+    pair_recv,
     hop_send,
     hop_recv,
 ):
@@ -154,9 +179,10 @@
         piece = kv.at[core, g, (bm, bp)[way], :, way]
         return remote(piece, piece, b_send.at[2 + way, g], b_recv.at[2 + way, g], (dev_bp, dev_bm)[way])
 
-    def across(g, which):
-        piece = kv.at[core, g, (b, bm, bp, bo)[which]]
-        return remote(piece, piece, s_send.at[which, g], s_recv.at[which, g], dev_sib)
+    mine, theirs = pl.ds(0, ROWS), pl.ds(ROWS, ROWS)
+    q_across = remote(q_rows.at[mine], q_rows.at[theirs], pair_send.at[0], pair_recv.at[0], dev_sib)
+    acc_across = remote(acc_out, acc_in, pair_send.at[1], pair_recv.at[1], dev_sib)
+    stat_across = remote(stat_out, stat_in, pair_send.at[2], pair_recv.at[2], dev_sib)
 
     def hop(n):
         which, group, half = HOPS[n]
@@ -167,11 +193,6 @@
         device = along_z[-1 if which == 0 else 1]
         return source_group, remote(source, target, hop_send.at[n], hop_recv.at[n], device)
 
-    def across_hopped(g):
-        piece = kv.at[core, g]
-        n = g - GROUPS
-        return remote(piece, piece, s_send.at[4, n], s_recv.at[4, n], dev_sib)
-
     for move in starts:
         move.start()
 
@@ -199,33 +220,21 @@
             a_on(g, way).wait_recv()
         for way in (0, 1):
             row_out(g, way).start()
-        across(g, 0).start()
 
     def stage_b1(g):
         for way in (0, 1):
             row_out(g, way).wait_recv()
             b_on(g, way).start()
-            across(g, 1 + way).start()
 
     def stage_b2(g):
         for way in (0, 1):
             b_on(g, way).wait_recv()
-        across(g, 3).start()
         for n in range(len(HOPS)):
             source_group, copy = hop(n)
 
             @pl.when(g == source_group)
             def _(copy=copy):
                 copy.start()
-
-    def stage_hopped(g):
-        for n, (_, group, _) in enumerate(HOPS):
-
-            @pl.when(g == group)
-            def _(n=n):
-                hop(n)[1].wait_recv()
-
-        across_hopped(g).start()
 
     def select(g, half):
         value = jnp.int32(0)
@@ -237,41 +246,42 @@
         if step < 2:
             q_copies[step].wait()
             q_rows[step * LAYER_ROWS : (step + 1) * LAYER_ROWS] = q_in[step].reshape(LAYER_ROWS, WIDTH)
-        elif step == 2:
-            row_max[...] = jnp.full_like(row_max, FLOOR)
-            row_sum[...] = jnp.zeros_like(row_sum)
+            if step == 1:
+                q_across.start()
         else:
-            acc[...] = jnp.zeros_like(acc)
-
-    def attend(g, layer, last):
+            part = pl.ds((step - 2) * ROWS, ROWS)
+            acc[part] = jnp.zeros((ROWS, WIDTH), jnp.float32)
+            row_max[part] = jnp.full((ROWS, 128), FLOOR, jnp.float32)
+            row_sum[part] = jnp.zeros((ROWS, 128), jnp.float32)
+
+    def attend(g, layer, token_block, last):
         def keys_of(which):
             pieces = []
             for x_key in range(last + 1):
-                pieces.append(kv[0, g, :, x_key, which].reshape(HALF, WIDTH))
-                pieces.append(kv[1, g, x_key, :, which].reshape(HALF, WIDTH))
+                for y_key in range(SIDE):
+                    row = y_key * flip + x_key * core
+                    column = x_key * flip + y_key * core
+                    pieces.append(kv[core, g, row, column, which])
             return jnp.concatenate(pieces, axis=0)
 
         keys = keys_of(0)
         values = keys_of(1)
-        at = lax.broadcasted_iota(jnp.int32, (1, 2 * HALF), 1)
-        from_core = at // HALF
-        y_key = lax.rem(at // GROUP_ROWS, SIDE)
+        at = lax.broadcasted_iota(jnp.int32, (1, HALF), 1)
+        y_key = at // GROUP_ROWS
         z_rel = jnp.where(lax.rem(at // SHARD, 2) == 0, select(g, 0), select(g, 1))
         z_key = lax.rem(z + z_rel + DEPTH, DEPTH)
-        key_pos = ((last * SIDE + y_key) * 2 + from_core) * BLOCK + z_key * SHARD + lax.rem(at, SHARD)
-        open_width = 2 * HALF * last
-        lanes = 2 * (last + 1)
+        key_pos = ((last * SIDE + y_key) * 2 + core) * BLOCK + z_key * SHARD + lax.rem(at, SHARD)
+        open_width = HALF * last
         start = layer * LAYER_ROWS
         for tile in range(LAYER_ROWS // TILE):
-            here = pl.ds(pl.multiple_of(start + tile * TILE, TILE), TILE)
+            here = pl.ds(start + tile * TILE, TILE)
             scores = lax.dot_general(
                 q_rows[here], keys, (((1,), (1,)), ((), ())), preferred_element_type=jnp.float32
             )
             row = lax.broadcasted_iota(jnp.int32, (TILE, 1), 0) + tile * TILE
-            allowed = key_pos <= place * BLOCK + row // 2
+            allowed = key_pos <= token_block * BLOCK + row // 2
             edge = jnp.where(allowed, scores[:, open_width:], MASKED)
-            pieces = [scores[:, n * 128 : (n + 1) * 128] for n in range(lanes - 2)]
-            pieces += [edge[:, :128], edge[:, 128:]]
+            pieces = [scores[:, n * HALF : (n + 1) * HALF] for n in range(last)] + [edge]
             peak = functools.reduce(jnp.maximum, pieces)
             old = row_max[here]
             new = jnp.maximum(old, jnp.max(peak, axis=1, keepdims=True))
@@ -283,17 +293,30 @@
             mixed = jnp.dot(rounded, values, preferred_element_type=jnp.float32)
             acc[here] = acc[here] * jnp.concatenate((fade, fade), axis=1) + mixed
 
-    def use(g, layer):
+    def use(g, rows):
+        token_block = place if rows == MINE else place + 1 - 2 * core
         for last in range(SIDE):
 
             @pl.when(x == last)
             def _(last=last):
-                attend(g, layer, last)
-
-    def stage_use(g):
-        for which in range(4):
-            across(g, which).wait_recv()
-        use(g, 0)
+                for layer in (2 * rows, 2 * rows + 1):
+                    attend(g, layer, token_block, last)
+
+    row_at = lax.broadcasted_iota(jnp.int32, (128, 128), 0)
+    diagonal = row_at == lax.broadcasted_iota(jnp.int32, (128, 128), 1)
+
+    def hand_over():
+        acc_out[...] = acc[theirs].astype(jnp.bfloat16)
+        acc_across.start()
+        count = ROWS // 128
+        for block in range(count):
+            there = pl.ds(ROWS + block * 128, 128)
+            total = jnp.sum(row_sum[there], axis=1, keepdims=True)
+            for n, value in ((block, row_max[there]), (count + block, total)):
+                stat_out[n : n + 1] = jnp.sum(
+                    jnp.where(diagonal, value, 0.0), axis=0, keepdims=True
+                )
+        stat_across.start()
 
     def drain(g):
         for way in (0, 1):
@@ -301,18 +324,22 @@
             a_on(g, way).wait_send()
             row_out(g, way).wait_send()
             b_on(g, way).wait_send()
-        for which in range(4):
-            across(g, which).wait_send()
 
     stages = (
         (OFF_OWN, stage_own),
         (OFF_A1, stage_a1),
         (OFF_A2, stage_a2),
-        (OFF_USE, stage_use),
         (OFF_B1, stage_b1),
         (OFF_B2, stage_b2),
     )
-    hop_tick = TICKS - len(HOPPED)
+
+    def pick(index, table):
+        value = jnp.int32(0)
+        for n, entry in enumerate(table):
+            value = jnp.where(index == n, entry, value)
+        return value
+
+    begins = [sum(tick < at for tick, _, _ in ITEMS) for at in range(TICKS + 1)]
 
     @pl.loop(0, TICKS)
     def _(tick):
@@ -329,40 +356,59 @@
             def _(step=step):
                 prepare(step)
 
-        hopped = tick >= hop_tick
-        hop_group = jnp.where(hopped, tick - hop_tick + GROUPS, GROUPS)
-
-        @pl.when(hopped)
-        def _():
-            stage_hopped(hop_group)
-
-        @pl.loop(0, jnp.where(hopped, 3, jnp.where(tick >= OFF_USE, 1, 0)))
+        @pl.loop(pick(tick, begins), pick(tick + 1, begins))
         def _(item):
-            @pl.when(item == 1)
+            @pl.when(item == 0)
             def _():
-                across_hopped(hop_group).wait_recv()
-                use(hop_group, 0)
-
-            @pl.when(item != 1)
+                q_across.wait_recv()
+
+            for n, (_, group, _) in enumerate(HOPS):
+
+                @pl.when(item == ITEMS.index((8 if group == GROUPS else 9, group, SIBLING)))
+                def _(n=n):
+                    hop(n)[1].wait_recv()
+
+            @pl.when(item == HAND_OVER)
             def _():
-                use(jnp.where(item == 0, tick - OFF_USE, hop_group), 1)
+                hand_over()
+
+            group = pick(item, [group for _, group, _ in ITEMS])
+            rows = pick(item, [rows for _, _, rows in ITEMS])
+            for choice in (MINE, SIBLING):
+
+                @pl.when(rows == choice)
+                def _(choice=choice):
+                    use(group, choice)
 
     for move in arrivals.values():
         move.wait_send()
     for n in range(len(HOPS)):
         hop(n)[1].wait_send()
-    for g in range(GROUPS, len(RELATIVE)):
-        across_hopped(g).wait_send()
+    q_across.wait_send()
 
     @pl.loop(0, GROUPS)
     def _(g):
         drain(g)
 
+    stat_across.wait()
+    acc_across.wait()
+    count = ROWS // 128
     for layer, o_ref in enumerate((o1_ref, o2_ref)):
-        for part in range(LAYER_ROWS // TILE):
-            here = pl.ds(layer * LAYER_ROWS + part * TILE, TILE)
-            inverse = 1.0 / jnp.sum(row_sum[here], axis=1, keepdims=True)
-            o_ref[part * TILE : (part + 1) * TILE] = (acc[here] * inverse).astype(jnp.bfloat16)
+        for part in range(LAYER_ROWS // 128):
+            block = layer * (LAYER_ROWS // 128) + part
+            here = pl.ds(block * 128, 128)
+
+            def column(n):
+                return jnp.sum(jnp.where(diagonal, stat_in[n : n + 1], 0.0), axis=1, keepdims=True)
+
+            own_max, other_max = row_max[here][:, :1], column(block)
+            peak = jnp.maximum(own_max, other_max)
+            keep = jnp.exp2((own_max - peak) * scale2)
+            add = jnp.exp2((other_max - peak) * scale2)
+            total = jnp.sum(row_sum[here], axis=1, keepdims=True) * keep + column(count + block) * add
+            inverse = 1.0 / total
+            result = acc[here] * (keep * inverse) + acc_in[here].astype(jnp.float32) * (add * inverse)
+            o_ref[part * 128 : (part + 1) * 128] = result.astype(jnp.bfloat16)
 
 
 def on_device(queries_first, queries_second, shared_keys, shared_values):
@@ -380,10 +426,14 @@
         scratch_shapes=[
             pltpu.VMEM((2, len(RELATIVE), SIDE, SIDE, 2, GROUP_ROWS, width), jnp.bfloat16),
             pltpu.VMEM((2, tokens_here, heads, width), jnp.bfloat16),
+            pltpu.VMEM((2 * rows, width), jnp.bfloat16),
+            pltpu.VMEM((2 * rows, 128), jnp.float32),
+            pltpu.VMEM((2 * rows, 128), jnp.float32),
+            pltpu.VMEM((2 * rows, width), jnp.float32),
             pltpu.VMEM((rows, width), jnp.bfloat16),
-            pltpu.VMEM((rows, 128), jnp.float32),
-            pltpu.VMEM((rows, 128), jnp.float32),
-            pltpu.VMEM((rows, width), jnp.float32),
+            pltpu.VMEM((rows, width), jnp.bfloat16),
+            pltpu.VMEM((2 * rows // 128, 128), jnp.float32),
+            pltpu.VMEM((2 * rows // 128, 128), jnp.float32),
             dma((4,)),
             dma((GROUPS, 2)),
             dma((GROUPS, 2)),
@@ -391,8 +441,8 @@
             dma((4, GROUPS)),
             dma((4, GROUPS)),
             dma((4, GROUPS)),
-            dma((5, GROUPS)),
-            dma((5, GROUPS)),
+            dma((3,)),
+            dma((3,)),
             dma((len(HOPS),)),
             dma((len(HOPS),)),
         ],

time: 64.3 us -> 64 us (level)
  no operation moved by 1% of the time
where the time goes in v4:
time: 64 us; the launch traced here: 63.8 us
  Pallas kernels  60.6 us (95%)
  local copies, waits for them, and re-layouts  2.6 us (4%)
  between operations  0.65 us (1%)
    pallas_call x1, Pallas kernels, on_device(): pl.pallas_call(functools.partial(attention_kernel, scale2), out_shape=(ou...  60.6 us
    reshape x2, local copies, waits for them, and re-layouts, on_device(): return tuple((array.reshape(tokens_here, heads, width) for array in result))  2.6 us

profile of v4, /device:TPU:6, one launch (start us, length us, event | category | flops | bytes accessed | tf_op | source)
XLA Modules:
  0.0 63.8 jit_solution(15162913227638741664)
XLA Ops:
  0.6 60.6 %shard_map.59 = (bf16[512,256]{1,0:T(8,128)(2,1)}, bf16[512,256]{1,0:T(8,128)(2,1)}) custom-call(bf16[256,2,256]{2,1,0:T(2,128)(2,1)} %q1_hbm.1, bf16[256,2,256]{2,1,0:T(2,128)(2,1)} %q2_hbm.1, bf16[16,256]{1,0:T(8,128)(2,1)} %k_hbm.1, bf16[16,256]{1,0:T(8,128)(2,1)} %v_hbm.1), custom_call_target="tpu_custom_call" | custom-call | flops 8589934592 | bytes 1048576 | tf_op jit(solution)/shard_map/pallas_call | solution.py:421
  61.2 0.0 copy-start
  61.2 1.8 %reshape.10 = bf16[256,2,256]{2,1,0:T(2,128)(2,1)} reshape(bf16[512,256]{1,0:T(8,128)(2,1)} %get-tuple-element.4) | data formatting | bytes 524288 | tf_op jit(solution)/shard_map/reshape | solution.py:456
  63.0 0.0 copy-done
  63.0 0.8 %reshape.11 = bf16[256,2,256]{2,1,0:T(2,128)(2,1)} reshape(bf16[512,256]{1,0:T(8,128)(2,1)S(1)} %copy-done) | data formatting | bytes 524288 | tf_op jit(solution)/shard_map/reshape | solution.py:456
Async XLA Ops:
  61.2 1.8 %copy-start = (bf16[512,256]{1,0:T(8,128)(2,1)S(1)}, bf16[512,256]{1,0:T(8,128)(2,1)}, u32[]{:S(2)}) copy-start(bf16[512,256]{1,0:T(8,128)(2,1)} %get-tuple-element.5) | copy-start | bytes 786436

commit v5 on v4

--- a/solution.py
+++ b/solution.py
@@ -31,28 +31,28 @@
     for half in (0, 1)
 )
 ONWARD = ((1, -2, 3), (-1, 2, -3), (3, -2, 5), (-3, 2, -5), (5, -2, 7), (-5, 2, -7), (7, -1, 8))
-OFF_OWN, OFF_A1, OFF_A2, OFF_B1, OFF_B2 = 0, 1, 2, 3, 4
-TICKS = GROUPS + OFF_B2
+OFF_OWN, OFF_A1, OFF_A2, OFF_B1, OFF_B2 = 0, 1, 2, 4, 5
+TICKS = GROUPS + OFF_B2 + 1
 MINE, SIBLING = 0, 1
 ITEMS = (
-    (4, 0, SIBLING),
-    (5, 1, SIBLING),
-    (5, 0, MINE),
-    (6, 2, SIBLING),
-    (6, 1, MINE),
-    (7, 3, SIBLING),
-    (7, 2, MINE),
-    (8, 4, SIBLING),
-    (8, 3, MINE),
-    (8, 6, SIBLING),
-    (8, 6, MINE),
-    (9, 5, SIBLING),
-    (9, 7, SIBLING),
-    (9, 4, MINE),
-    (9, 5, MINE),
-    (9, 7, MINE),
+    (6, 0, SIBLING),
+    (7, 1, SIBLING),
+    (7, 0, MINE),
+    (8, 2, SIBLING),
+    (8, 1, MINE),
+    (9, 3, SIBLING),
+    (9, 2, MINE),
+    (10, 4, SIBLING),
+    (10, 3, MINE),
+    (10, 6, SIBLING),
+    (10, 4, MINE),
+    (10, 6, MINE),
+    (10, 7, SIBLING),
+    (11, 5, SIBLING),
+    (11, 7, MINE),
+    (11, 5, MINE),
 )
-HAND_OVER = 13
+HAND_OVER = 14
 TILE = 256
 
 
@@ -327,10 +327,10 @@
 
     stages = (
         (OFF_OWN, stage_own),
+        (OFF_B1, stage_b1),
         (OFF_A1, stage_a1),
+        (OFF_B2, stage_b2),
         (OFF_A2, stage_a2),
-        (OFF_B1, stage_b1),
-        (OFF_B2, stage_b2),
     )
 
     def pick(index, table):
@@ -343,19 +343,6 @@
 
     @pl.loop(0, TICKS)
     def _(tick):
-        for offset, stage in stages:
-            g = tick - offset
-
-            @pl.when((g >= 0) & (g < GROUPS))
-            def _(stage=stage, g=g):
-                stage(g)
-
-        for step in range(4):
-
-            @pl.when(tick == step)
-            def _(step=step):
-                prepare(step)
-
         @pl.loop(pick(tick, begins), pick(tick + 1, begins))
         def _(item):
             @pl.when(item == 0)
@@ -364,7 +351,7 @@
 
             for n, (_, group, _) in enumerate(HOPS):
 
-                @pl.when(item == ITEMS.index((8 if group == GROUPS else 9, group, SIBLING)))
+                @pl.when(item == ITEMS.index((10, group, SIBLING)))
                 def _(n=n):
                     hop(n)[1].wait_recv()
 
@@ -379,6 +366,19 @@
                 @pl.when(rows == choice)
                 def _(choice=choice):
                     use(group, choice)
+
+        for offset, stage in stages:
+            g = tick - offset
+
+            @pl.when((g >= 0) & (g < GROUPS))
+            def _(stage=stage, g=g):
+                stage(g)
+
+        for step in range(4):
+
+            @pl.when(tick == step)
+            def _(step=step):
+                prepare(step)
 
     for move in arrivals.values():
         move.wait_send()

time: 64 us -> 62.1 us (0.970)
  Pallas kernels: 60.6 us -> 58.7 us
    pallas_call x1, Pallas kernels: 60.6 us -> 58.7 us  [on_device(): pl.pallas_call(functools.partial(attention_kernel, scale2), out_shape=(ou...]
where the time goes in v5:
time: 62.1 us; the launch traced here: 62 us
  Pallas kernels  58.7 us (95%)
  local copies, waits for them, and re-layouts  2.6 us (4%)
  between operations  0.65 us (1%)
    pallas_call x1, Pallas kernels, on_device(): pl.pallas_call(functools.partial(attention_kernel, scale2), out_shape=(ou...  58.7 us
    reshape x2, local copies, waits for them, and re-layouts, on_device(): return tuple((array.reshape(tokens_here, heads, width) for array in result))  2.6 us

profile of v5, /device:TPU:6, one launch (start us, length us, event | category | flops | bytes accessed | tf_op | source)
XLA Modules:
  0.0 62.0 jit_solution(264911412652507865)
XLA Ops:
  0.6 58.7 %shard_map.59 = (bf16[512,256]{1,0:T(8,128)(2,1)}, bf16[512,256]{1,0:T(8,128)(2,1)}) custom-call(bf16[256,2,256]{2,1,0:T(2,128)(2,1)} %q1_hbm.1, bf16[256,2,256]{2,1,0:T(2,128)(2,1)} %q2_hbm.1, bf16[16,256]{1,0:T(8,128)(2,1)} %k_hbm.1, bf16[16,256]{1,0:T(8,128)(2,1)} %v_hbm.1), custom_call_target="tpu_custom_call" | custom-call | flops 8589934592 | bytes 1048576 | tf_op jit(solution)/shard_map/pallas_call | solution.py:421
  59.4 0.0 copy-start
  59.4 1.8 %reshape.10 = bf16[256,2,256]{2,1,0:T(2,128)(2,1)} reshape(bf16[512,256]{1,0:T(8,128)(2,1)} %get-tuple-element.4) | data formatting | bytes 524288 | tf_op jit(solution)/shard_map/reshape | solution.py:456
  61.2 0.0 copy-done
  61.2 0.8 %reshape.11 = bf16[256,2,256]{2,1,0:T(2,128)(2,1)} reshape(bf16[512,256]{1,0:T(8,128)(2,1)S(1)} %copy-done) | data formatting | bytes 524288 | tf_op jit(solution)/shard_map/reshape | solution.py:456
Async XLA Ops:
  59.4 1.8 %copy-start = (bf16[512,256]{1,0:T(8,128)(2,1)S(1)}, bf16[512,256]{1,0:T(8,128)(2,1)}, u32[]{:S(2)}) copy-start(bf16[512,256]{1,0:T(8,128)(2,1)} %get-tuple-element.5) | copy-start | bytes 786436

commit v6 on v5

--- a/solution.py
+++ b/solution.py
@@ -70,8 +70,7 @@
     q2_hbm,
     k_hbm,
     v_hbm,
-    o1_ref,
-    o2_ref,
+    o_ref,
     kv,
     q_in,
     q_rows,
@@ -254,7 +253,7 @@
             row_max[part] = jnp.full((ROWS, 128), FLOOR, jnp.float32)
             row_sum[part] = jnp.zeros((ROWS, 128), jnp.float32)
 
-    def attend(g, layer, token_block, last):
+    def attend(g, rows, token_block, last):
         def keys_of(which):
             pieces = []
             for x_key in range(last + 1):
@@ -272,26 +271,44 @@
         z_key = lax.rem(z + z_rel + DEPTH, DEPTH)
         key_pos = ((last * SIDE + y_key) * 2 + core) * BLOCK + z_key * SHARD + lax.rem(at, SHARD)
         open_width = HALF * last
-        start = layer * LAYER_ROWS
-        for tile in range(LAYER_ROWS // TILE):
-            here = pl.ds(start + tile * TILE, TILE)
-            scores = lax.dot_general(
-                q_rows[here], keys, (((1,), (1,)), ((), ())), preferred_element_type=jnp.float32
+        tiles = [pl.ds(rows * ROWS + n * TILE, TILE) for n in range(ROWS // TILE)]
+        scores, weights, fades = {}, {}, {}
+
+        def score_tile(n):
+            scores[n] = lax.dot_general(
+                q_rows[tiles[n]], keys, (((1,), (1,)), ((), ())), preferred_element_type=jnp.float32
             )
-            row = lax.broadcasted_iota(jnp.int32, (TILE, 1), 0) + tile * TILE
+
+        def soften_tile(n):
+            here = tiles[n]
+            tile_scores = scores.pop(n)
+            row = lax.broadcasted_iota(jnp.int32, (TILE, 1), 0) + (n * TILE) % LAYER_ROWS
             allowed = key_pos <= token_block * BLOCK + row // 2
-            edge = jnp.where(allowed, scores[:, open_width:], MASKED)
-            pieces = [scores[:, n * HALF : (n + 1) * HALF] for n in range(last)] + [edge]
+            edge = jnp.where(allowed, tile_scores[:, open_width:], MASKED)
+            pieces = [tile_scores[:, i * HALF : (i + 1) * HALF] for i in range(last)] + [edge]
             peak = functools.reduce(jnp.maximum, pieces)
             old = row_max[here]
             new = jnp.maximum(old, jnp.max(peak, axis=1, keepdims=True))
             fade = jnp.exp2((old - new) * scale2)
-            weights = [jnp.exp2((piece - new) * scale2) for piece in pieces]
+            parts = [jnp.exp2((piece - new) * scale2) for piece in pieces]
             row_max[here] = new
-            row_sum[here] = row_sum[here] * fade + functools.reduce(jnp.add, weights)
-            rounded = jnp.concatenate([w.astype(jnp.bfloat16) for w in weights], axis=1)
-            mixed = jnp.dot(rounded, values, preferred_element_type=jnp.float32)
-            acc[here] = acc[here] * jnp.concatenate((fade, fade), axis=1) + mixed
+            row_sum[here] = row_sum[here] * fade + functools.reduce(jnp.add, parts)
+            weights[n] = jnp.concatenate([part.astype(jnp.bfloat16) for part in parts], axis=1)
+            fades[n] = fade
+
+        def mix_tile(n):
+            here = tiles[n]
+            mixed = jnp.dot(weights.pop(n), values, preferred_element_type=jnp.float32)
+            acc[here] = acc[here] * jnp.concatenate((fades[n], fades[n]), axis=1) + mixed
+
+        score_tile(0)
+        for n in range(len(tiles)):
+            if n + 1 < len(tiles):
+                score_tile(n + 1)
+            if n:
+                mix_tile(n - 1)
+            soften_tile(n)
+        mix_tile(len(tiles) - 1)
 
     def use(g, rows):
         token_block = place if rows == MINE else place + 1 - 2 * core
@@ -299,8 +316,7 @@
 
             @pl.when(x == last)
             def _(last=last):
-                for layer in (2 * rows, 2 * rows + 1):
-                    attend(g, layer, token_block, last)
+                attend(g, rows, token_block, last)
 
     row_at = lax.broadcasted_iota(jnp.int32, (128, 128), 0)
     diagonal = row_at == lax.broadcasted_iota(jnp.int32, (128, 128), 1)
@@ -393,7 +409,7 @@
     stat_across.wait()
     acc_across.wait()
     count = ROWS // 128
-    for layer, o_ref in enumerate((o1_ref, o2_ref)):
+    for layer in range(2):
         for part in range(LAYER_ROWS // 128):
             block = layer * (LAYER_ROWS // 128) + part
             here = pl.ds(block * 128, 128)
@@ -408,7 +424,8 @@
             total = jnp.sum(row_sum[here], axis=1, keepdims=True) * keep + column(count + block) * add
             inverse = 1.0 / total
             result = acc[here] * (keep * inverse) + acc_in[here].astype(jnp.float32) * (add * inverse)
-            o_ref[part * 128 : (part + 1) * 128] = result.astype(jnp.bfloat16)
+            tokens = slice(part * 64, (part + 1) * 64)
+            o_ref[tokens, 2 * layer : 2 * layer + 2] = result.astype(jnp.bfloat16).reshape(64, 2, WIDTH)
 
 
 def on_device(queries_first, queries_second, shared_keys, shared_values):
@@ -416,13 +433,13 @@
     rows = 2 * tokens_here * heads
     scale2 = math.log2(math.e) / math.sqrt(width)
     dma = pltpu.SemaphoreType.DMA
-    out = jax.ShapeDtypeStruct((rows // 2, width), jnp.bfloat16)
+    out = jax.ShapeDtypeStruct((tokens_here, 2 * heads, width), jnp.bfloat16)
     vmem = pl.BlockSpec(memory_space=pltpu.VMEM)
     result = pl.pallas_call(
         functools.partial(attention_kernel, scale2),
-        out_shape=(out, out),
+        out_shape=out,
         in_specs=[pl.BlockSpec(memory_space=pl.ANY)] * 4,
-        out_specs=(vmem, vmem),
+        out_specs=vmem,
         scratch_shapes=[
             pltpu.VMEM((2, len(RELATIVE), SIDE, SIDE, 2, GROUP_ROWS, width), jnp.bfloat16),
             pltpu.VMEM((2, tokens_here, heads, width), jnp.bfloat16),
@@ -453,7 +470,7 @@
             flops=4 * rows * 8192 * width, bytes_accessed=1 << 20, transcendentals=rows * 8192
         ),
     )(queries_first, queries_second, shared_keys, shared_values)
-    return tuple(array.reshape(tokens_here, heads, width) for array in result)
+    return result[:, :heads], result[:, heads:]
 
 
 def solution(mesh):

time: 62.1 us -> 61.7 us (level)
    reshape x2 -> x0, local copies, waits for them, and re-layouts: 2.6 us -> none  [on_device(): return tuple((array.reshape(tokens_here, heads, width) for array in result))]
    slice x0 -> x1, local copies, waits for them, and re-layouts: none -> 2.44 us  [on_device(): return (result[:, :heads], result[:, heads:])]
where the time goes in v6:
time: 61.7 us; the launch traced here: 61.5 us
  Pallas kernels  58.5 us (95%)
  local copies, waits for them, and re-layouts  2.44 us (4%)
  between operations  0.64 us (1%)
    pallas_call x1, Pallas kernels, on_device(): pl.pallas_call(functools.partial(attention_kernel, scale2), out_shape=out...  58.5 us
    slice x1, local copies, waits for them, and re-layouts, on_device(): return (result[:, :heads], result[:, heads:])  2.44 us

profile of v6, /device:TPU:6, one launch (start us, length us, event | category | flops | bytes accessed | tf_op | source)
XLA Modules:
  0.0 61.5 jit_solution(15478044106476840028)
XLA Ops:
  0.6 58.5 %shard_map.59 = bf16[256,4,256]{2,1,0:T(4,128)(2,1)} custom-call(bf16[256,2,256]{2,1,0:T(2,128)(2,1)} %q1_hbm.1, bf16[256,2,256]{2,1,0:T(2,128)(2,1)} %q2_hbm.1, bf16[16,256]{1,0:T(8,128)(2,1)} %k_hbm.1, bf16[16,256]{1,0:T(8,128)(2,1)} %v_hbm.1), custom_call_target="tpu_custom_call" | custom-call | flops 8589934592 | bytes 1048576 | tf_op jit(solution)/shard_map/pallas_call | solution.py:438
  59.1 2.4 %fusion = (bf16[256,2,256]{2,1,0:T(2,128)(2,1)}, bf16[256,2,256]{2,1,0:T(2,128)(2,1)}) fusion(bf16[256,4,256]{2,1,0:T(4,128)(2,1)} %shard_map.59), kind=kLoop, calls=%fused_computation | loop fusion | bytes 1048576 | tf_op jit(solution)/shard_map/slice | solution.py:473

commit v7 on v6

--- a/solution.py
+++ b/solution.py
@@ -36,18 +36,18 @@
 MINE, SIBLING = 0, 1
 ITEMS = (
     (6, 0, SIBLING),
+    (6, 0, MINE),
     (7, 1, SIBLING),
-    (7, 0, MINE),
+    (7, 1, MINE),
     (8, 2, SIBLING),
-    (8, 1, MINE),
+    (8, 2, MINE),
     (9, 3, SIBLING),
-    (9, 2, MINE),
+    (9, 3, MINE),
+    (9, 6, SIBLING),
+    (9, 6, MINE),
     (10, 4, SIBLING),
-    (10, 3, MINE),
-    (10, 6, SIBLING),
+    (10, 7, SIBLING),
     (10, 4, MINE),
-    (10, 6, MINE),
-    (10, 7, SIBLING),
     (11, 5, SIBLING),
     (11, 7, MINE),
     (11, 5, MINE),
@@ -367,7 +367,7 @@
 
             for n, (_, group, _) in enumerate(HOPS):
 
-                @pl.when(item == ITEMS.index((10, group, SIBLING)))
+                @pl.when(item == ITEMS.index((9 if group == GROUPS else 10, group, SIBLING)))
                 def _(n=n):
                     hop(n)[1].wait_recv()
 

time: 61.7 us -> 60.3 us (0.977)
  Pallas kernels: 58.5 us -> 57.1 us
    pallas_call x1, Pallas kernels: 58.5 us -> 57.1 us  [on_device(): pl.pallas_call(functools.partial(attention_kernel, scale2), out_shape=out...]
where the time goes in v7:
time: 60.3 us; the launch traced here: 60.2 us
  Pallas kernels  57.1 us (95%)
  local copies, waits for them, and re-layouts  2.44 us (4%)
  between operations  0.64 us (1%)
    pallas_call x1, Pallas kernels, on_device(): pl.pallas_call(functools.partial(attention_kernel, scale2), out_shape=out...  57.1 us
    slice x1, local copies, waits for them, and re-layouts, on_device(): return (result[:, :heads], result[:, heads:])  2.44 us

profile of v7, /device:TPU:6, one launch (start us, length us, event | category | flops | bytes accessed | tf_op | source)
XLA Modules:
  0.0 60.2 jit_solution(11316809453355627645)
XLA Ops:
  0.6 57.1 %shard_map.59 = bf16[256,4,256]{2,1,0:T(4,128)(2,1)} custom-call(bf16[256,2,256]{2,1,0:T(2,128)(2,1)} %q1_hbm.1, bf16[256,2,256]{2,1,0:T(2,128)(2,1)} %q2_hbm.1, bf16[16,256]{1,0:T(8,128)(2,1)} %k_hbm.1, bf16[16,256]{1,0:T(8,128)(2,1)} %v_hbm.1), custom_call_target="tpu_custom_call" | custom-call | flops 8589934592 | bytes 1048576 | tf_op jit(solution)/shard_map/pallas_call | solution.py:438
  57.7 2.4 %fusion = (bf16[256,2,256]{2,1,0:T(2,128)(2,1)}, bf16[256,2,256]{2,1,0:T(2,128)(2,1)}) fusion(bf16[256,4,256]{2,1,0:T(4,128)(2,1)} %shard_map.59), kind=kLoop, calls=%fused_computation | loop fusion | bytes 1048576 | tf_op jit(solution)/shard_map/slice | solution.py:473

commit v8 on v7

--- a/solution.py
+++ b/solution.py
@@ -46,14 +46,14 @@
     (9, 6, SIBLING),
     (9, 6, MINE),
     (10, 4, SIBLING),
+    (10, 4, MINE),
     (10, 7, SIBLING),
-    (10, 4, MINE),
     (11, 5, SIBLING),
     (11, 7, MINE),
     (11, 5, MINE),
 )
 HAND_OVER = 14
-TILE = 256
+TILE = 512
 
 
 def place_of(relative):

time: 60.3 us -> 59.7 us (0.990)
    pallas_call x1, Pallas kernels: 57.1 us -> 56.5 us  [on_device(): pl.pallas_call(functools.partial(attention_kernel, scale2), out_shape=out...]
where the time goes in v8:
time: 59.7 us; the launch traced here: 59.6 us
  Pallas kernels  56.5 us (95%)
  local copies, waits for them, and re-layouts  2.44 us (4%)
  between operations  0.64 us (1%)
    pallas_call x1, Pallas kernels, on_device(): pl.pallas_call(functools.partial(attention_kernel, scale2), out_shape=out...  56.5 us
    slice x1, local copies, waits for them, and re-layouts, on_device(): return (result[:, :heads], result[:, heads:])  2.44 us

profile of v8, /device:TPU:6, one launch (start us, length us, event | category | flops | bytes accessed | tf_op | source)
XLA Modules:
  0.0 59.6 jit_solution(13627290680339279129)
XLA Ops:
  0.6 56.5 %shard_map.59 = bf16[256,4,256]{2,1,0:T(4,128)(2,1)} custom-call(bf16[256,2,256]{2,1,0:T(2,128)(2,1)} %q1_hbm.1, bf16[256,2,256]{2,1,0:T(2,128)(2,1)} %q2_hbm.1, bf16[16,256]{1,0:T(8,128)(2,1)} %k_hbm.1, bf16[16,256]{1,0:T(8,128)(2,1)} %v_hbm.1), custom_call_target="tpu_custom_call" | custom-call | flops 8589934592 | bytes 1048576 | tf_op jit(solution)/shard_map/pallas_call | solution.py:438
  57.1 2.4 %fusion = (bf16[256,2,256]{2,1,0:T(2,128)(2,1)}, bf16[256,2,256]{2,1,0:T(2,128)(2,1)}) fusion(bf16[256,4,256]{2,1,0:T(4,128)(2,1)} %shard_map.59), kind=kLoop, calls=%fused_computation | loop fusion | bytes 1048576 | tf_op jit(solution)/shard_map/slice | solution.py:473
